TPU v7x, 32 devices: a whole 2x2x4 slice. The times are simulated.
32 devices in a mesh: seq: 32 (over z, y, x, core), dp: 1.
Axes of the slice: x: 2, y: 2, z: 4, core: 2. Of those that a mesh axis runs over, the one named last changes fastest.
Arguments:
- frames: bfloat16 [1, 4096, 1024], P('dp', 'seq'), may hold values from -36 to 36
- kernel: bfloat16 [31, 1024], replicated, may hold values from -1 to 1
- norm_gain: float32 [1024], replicated, may hold values from 0.5 to 1.5
- router: bfloat16 [1024, 8], replicated, may hold values from -0.1875 to 0.1875
- experts: int32 [1, 4096, 2], P('dp', 'seq'), may hold values from 0 to 7, all different within a row; in each aligned block of 128 rows (0 to 127, 128 to 255, ..., all dimensions but the last counted through in order) at most 64 rows name the same one
- w_in: bfloat16 [32, 1024, 512], P('seq'), may hold values from -0.1875 to 0.1875
- w_out: bfloat16 [32, 512, 1024], P('seq'), may hold values from -0.125 to 0.125
- cotangent: bfloat16 [1, 4096, 1024], P('dp', 'seq'), may hold values from -8 to 8
Outputs:
- mixed: bfloat16 [1, 4096, 1024], P('dp', 'seq')
- grad_frames: bfloat16 [1, 4096, 1024], P('dp', 'seq')
- grad_kernel: float32 [31, 1024], replicated
- grad_gain: float32 [1024], replicated
- grad_router: float32 [1024, 8], replicated
- grad_w_in: float32 [32, 1024, 512], P('seq')
- grad_w_out: float32 [32, 512, 1024], P('seq')
Inputs may be any that keep to these rules, and one draw needn't show every extreme that they name: Each frame names 2 different experts; in each aligned block of 128 frames no expert is named more than 64 times, a bound that some block reaches.
All inputs are finite; a program needn't handle non-finite values.
Results may differ from a plain program's by a relative error of at most 0.0075.
Values may be sent and summed in bfloat16 or wider, within the bound.
A program may use at most 128 MiB of HBM per device.

v0:
```python
import jax
import jax.numpy as jnp
from jax import lax
from jax.sharding import PartitionSpec as P

eps = 1e-06


def padded_2(shard, sides, width):
    for axis, dim in sides:
        size, length = (lax.axis_size(axis), shard.shape[dim])
        up = [(i, (i + 1) % size) for i in range(size - 1)]
        down = [(j, i) for i, j in up]
        last = lax.slice_in_dim(shard, length - width, length, axis=dim)
        initial = lax.slice_in_dim(shard, 0, width, axis=dim)
        before = lax.ppermute(last, axis, up)
        after = lax.ppermute(initial, axis, down)
        shard = jnp.concatenate([before, shard, after], axis=dim)
    return shard


def conv_forward(padded, kernel, row_count):
    summed = jnp.zeros((row_count, padded.shape[1]), jnp.float32)
    for offset in range(kernel.shape[0]):
        summed = summed + kernel[offset].astype(jnp.float32) * padded[
            offset : offset + row_count
        ].astype(jnp.float32)
    return summed


def conv_transpose(padded, kernel, row_count):
    length = kernel.shape[0]
    summed = jnp.zeros((row_count, padded.shape[1]), jnp.float32)
    for offset in range(length):
        start = length - 1 - offset
        summed = summed + kernel[offset].astype(jnp.float32) * padded[start : start + row_count]
    return summed


def kernel_terms(padded, upstream, length, row_count):
    return jnp.stack(
        [
            jnp.sum(padded[offset : offset + row_count].astype(jnp.float32) * upstream, axis=0)
            for offset in range(length)
        ]
    )


def normalize(summed, norm_gain):
    square = jnp.mean(summed * summed, axis=-1, keepdims=True)
    return summed * lax.rsqrt(square + eps) * norm_gain


def slot_numbers(expert_ids, expert_count):
    onehot = (expert_ids[:, None] == jnp.arange(expert_count, dtype=jnp.int32)[None, :]).astype(
        jnp.int32
    )
    ranks = jnp.cumsum(onehot, axis=0) - onehot
    return jnp.sum(ranks * onehot, axis=1)


def gate_values(normed_b, router, first_ids, second_ids):
    logits = jnp.dot(normed_b, router, preferred_element_type=jnp.float32)
    columns = jnp.arange(router.shape[1], dtype=jnp.int32)[None, :]
    pick_diff = (first_ids[:, None] == columns).astype(jnp.float32) - (
        second_ids[:, None] == columns
    ).astype(jnp.float32)
    gate_one = jax.nn.sigmoid(jnp.sum(logits * pick_diff, axis=1))
    return (gate_one, 1.0 - gate_one, pick_diff)


def swish_parts(pre_act):
    squash = jax.nn.sigmoid(pre_act)
    return (pre_act * squash, squash * (1.0 + pre_act * (1.0 - squash)))


def gate_backward(upstream, out_one, out_two, gate_one, gate_two, pick_diff, normed_b, router):
    grad_gap = (
        (jnp.sum(upstream * out_one, axis=1) - jnp.sum(upstream * out_two, axis=1))
        * gate_one
        * gate_two
    )
    grad_logits = (grad_gap[:, None] * pick_diff).astype(jnp.bfloat16)
    router_term = jnp.dot(normed_b.T, grad_logits, preferred_element_type=jnp.float32)
    normed_term = jnp.dot(grad_logits, router.T, preferred_element_type=jnp.float32)
    return (router_term, normed_term)


def combine_back(partial_rows):
    return lax.all_to_all(partial_rows, "seq", split_axis=0, concat_axis=0, tiled=True)


def body(frames, kernel, norm_gain, router, experts, w_in, w_out, cotangent):
    inputs_dev = frames[0]
    row_count = inputs_dev.shape[0]
    width = inputs_dev.shape[1]
    length = kernel.shape[0]
    half_width = length // 2
    expert_count = router.shape[1]
    top_count = experts.shape[2]
    capacity = 2 * row_count * top_count // expert_count
    group_size = lax.axis_size("seq") // expert_count
    in_weights = w_in[0]
    out_weights = w_out[0]
    padded = padded_2(inputs_dev, (("seq", 0),), half_width)
    summed = inputs_dev.astype(jnp.float32) + conv_forward(padded, kernel, row_count)
    normed_b = normalize(summed, norm_gain).astype(jnp.bfloat16)
    choice_ids = experts[0]
    gate_one, gate_two, pick_diff = gate_values(
        normed_b, router, choice_ids[:, 0], choice_ids[:, 1]
    )
    flat_ids = choice_ids.reshape(-1)
    slot_index = slot_numbers(flat_ids, expert_count)
    position = flat_ids * capacity + slot_index
    dispatch_table = (
        lax.broadcasted_iota(jnp.int32, (expert_count * capacity, flat_ids.shape[0]), 0)
        == position[None, :]
    ).astype(jnp.bfloat16)

    def pack(values):
        return jnp.dot(dispatch_table, values, preferred_element_type=jnp.float32).astype(
            jnp.bfloat16
        )

    def spread(values):
        return jnp.repeat(pack(values).reshape(expert_count, capacity, width), group_size, axis=0)

    def slice_totals(returned):
        totals = jnp.sum(
            returned.astype(jnp.float32).reshape(expert_count, group_size, capacity, width), axis=1
        )
        return totals.reshape(expert_count * capacity, width)

    def gather_back(totals):
        picked = jnp.take(totals, position, axis=0)
        return picked.reshape(row_count, top_count, width)

    repeated = jnp.repeat(normed_b, top_count, axis=0)
    upstream = cotangent[0].astype(jnp.float32)
    grad_assigned = jnp.stack([gate_one[:, None] * upstream, gate_two[:, None] * upstream], axis=1)
    grad_values = grad_assigned.reshape(row_count * top_count, width).astype(jnp.bfloat16)
    arrived = lax.all_to_all(spread(repeated), "seq", split_axis=0, concat_axis=0, tiled=True)
    flat_rows = arrived.reshape(-1, width)
    pre_act = jnp.dot(flat_rows, in_weights, preferred_element_type=jnp.float32)
    hidden = swish_parts(pre_act)[0].astype(jnp.bfloat16)
    partial_rows = jnp.dot(hidden, out_weights, preferred_element_type=jnp.float32).astype(
        jnp.bfloat16
    )
    results = (combine_back(partial_rows.reshape(arrived.shape)), arrived)
    arrived = results[1]
    assigned = gather_back(slice_totals(results[0]))
    out_one = assigned[:, 0]
    out_two = assigned[:, 1]
    mixed = (summed + gate_one[:, None] * out_one + gate_two[:, None] * out_two).astype(
        jnp.bfloat16
    )
    incoming = lax.all_to_all(spread(grad_values), "seq", split_axis=0, concat_axis=0, tiled=True)
    flat_rows = arrived.reshape(-1, width)
    flat_grads = incoming.reshape(-1, width)
    pre_act = jnp.dot(flat_rows, in_weights, preferred_element_type=jnp.float32)
    hidden_f, slope = swish_parts(pre_act)
    hidden = hidden_f.astype(jnp.bfloat16)
    grad_hidden = jnp.dot(flat_grads, out_weights.T, preferred_element_type=jnp.float32)
    grad_pre = (grad_hidden * slope).astype(jnp.bfloat16)
    out_term = jnp.dot(hidden.T, flat_grads, preferred_element_type=jnp.float32)
    in_term = jnp.dot(flat_rows.T, grad_pre, preferred_element_type=jnp.float32)
    grad_part = jnp.dot(grad_pre, in_weights.T, preferred_element_type=jnp.float32).astype(
        jnp.bfloat16
    )
    grad_totals = slice_totals(
        lax.all_to_all(
            grad_part.reshape(arrived.shape), "seq", split_axis=0, concat_axis=0, tiled=True
        )
    )
    normed_grads = jnp.sum(gather_back(grad_totals), axis=1)
    router_term, normed_term = gate_backward(
        upstream, out_one, out_two, gate_one, gate_two, pick_diff, normed_b, router
    )
    pullback = jax.vjp(normalize, summed, norm_gain)[1]
    summed_grad, gain_term = pullback(normed_grads + normed_term)
    upstream_total = upstream + summed_grad
    padded_grad = padded_2(upstream_total.astype(jnp.bfloat16), (("seq", 0),), half_width).astype(
        upstream_total.dtype
    )
    grad_frames = (upstream_total + conv_transpose(padded_grad, kernel, row_count)).astype(
        jnp.bfloat16
    )
    kernel_term = kernel_terms(padded, upstream_total, length, row_count)
    grad_kernel, grad_gain, grad_router = lax.psum(
        (kernel_term, gain_term, router_term), ("seq", "dp")
    )
    grad_in, grad_out = (
        lax.psum(in_term.astype(jnp.bfloat16), "dp").astype(jnp.float32),
        lax.psum(out_term.astype(jnp.bfloat16), "dp").astype(jnp.float32),
    )
    return (
        mixed[None],
        grad_frames[None],
        grad_kernel,
        grad_gain,
        grad_router,
        grad_in[None],
        grad_out[None],
    )


def solution(mesh):
    return jax.shard_map(
        body,
        mesh=mesh,
        in_specs=(
            P("dp", "seq", None),
            P(),
            P(),
            P(),
            P("dp", "seq", None),
            P("seq", None, None),
            P("seq", None, None),
            P("dp", "seq", None),
        ),
        out_specs=(
            P("dp", "seq", None),
            P("dp", "seq", None),
            P(),
            P(),
            P(),
            P("seq", None, None),
            P("seq", None, None),
        ),
        check_vma=False,
    )
```

profile of v0, /device:TPU:0, one launch (start us, length us, event | category | flops | bytes accessed | tf_op | source)
XLA Modules:
  0.0 610.0 jit_solution(13365193039712191310)
XLA Ops:
  7.2 0.9 slice_bitcast_fusion.1
  8.1 2.4 collective-permute-start
  10.4 1.3 collective-permute-start.1
  11.7 0.8 copy.15
  12.8 1.0 slice_convert_fusion.29
  13.9 1.2 slice_convert_fusion.30
  15.3 0.6 reduce-window.6
  16.7 9.4 %multiply_reduce_fusion.2 = (f32[128]{0:T(128)S(1)}, f32[128,1024]{1,0:T(8,128)S(1)}) fusion(bf16[15,1024]{1,0:T(8,128)(2,1)S(1)} %collective-permute-done.1, bf16[128,1024]{1,0:T(8,128)(2,1)} %bitcast.178, f32[1024]{0:T(1024)S(1)} %bitcast.209, f32[1024]{0:T(1024)S(1)} %bitcast.211, f32[1024]{0:T(1024)S(1)} %bitcast.215, f32[1024]{0:T(1024)S(1)} %bitcast.217, ...), kind=kLoop, calls=%fused_computation.262 | loop fusion | flops 24248192 | bytes 975360 | tf_op jit(solution)/shard_map/reduce_sum | solution.py:50
  26.4 0.6 copy-done.4
  27.0 0.8 multiply_convert_fusion.2
  29.4 102.7 %all_to_all.20 = bf16[32,64,1024]{2,1,0:T(8,128)(2,1)S(1)} all-to-all(bf16[32,64,1024]{2,1,0:T(8,128)(2,1)S(1)} %bitcast.174), channel_id=1, replica_groups=mesh['seq'=32,'dp'=1] {'seq'}, dimensions={0} | all-to-all | bytes 8388608 | tf_op jit(solution)/shard_map/all_to_all | solution.py:142
  132.1 2.0 copy-done.2
  134.1 2.4 fusion.8
  136.5 4.4 convolution_convert_fusion.1
  140.9 4.0 all-to-all-start.1
  145.2 93.5 %all-to-all-done.1 = bf16[32,64,1024]{2,1,0:T(8,128)(2,1)} async-done(((bf16[32,64,1024]{2,1,0:T(8,128)(2,1)}), bf16[32,64,1024]{2,1,0:T(8,128)(2,1)}, u32[]{:S(2)}, u32[]{:S(2)}) %all-to-all-start.1) | async-done | bytes 4194336 | tf_op jit(solution)/shard_map/all_to_all | solution.py:90
  238.7 3.4 convert_reduce_fusion.1
  242.1 2.0 gather_fusion
  244.2 1.4 broadcast_select_fusion.1
  245.5 0.6 reshape.207
  246.2 0.8 fusion.156
  247.0 0.8 copy-done.6
  247.8 1.2 fusion.78
  249.5 1.1 fusion.75
  250.7 0.5 copy.19
  252.5 97.3 %all_to_all.21 = bf16[32,64,1024]{2,1,0:T(8,128)(2,1)S(1)} all-to-all(bf16[32,64,1024]{2,1,0:T(8,128)(2,1)S(1)} %bitcast.175), channel_id=1, replica_groups=mesh['seq'=32,'dp'=1] {'seq'}, dimensions={0} | all-to-all | bytes 8388608 | tf_op jit(solution)/shard_map/all_to_all | solution.py:157
  349.8 3.4 multiply_convert_fusion
  353.2 4.3 convolution_convert_fusion
  357.6 3.8 all-to-all-start.3
  361.9 6.0 fusion.1
  367.9 3.7 fusion.3
  371.6 83.7 %all-to-all-done.3 = bf16[32,64,1024]{2,1,0:T(8,128)(2,1)} async-done(((bf16[32,64,1024]{2,1,0:T(8,128)(2,1)}), bf16[32,64,1024]{2,1,0:T(8,128)(2,1)}, u32[]{:S(2)}, u32[]{:S(2)}) %all-to-all-start.3) | async-done | bytes 4194336 | tf_op jit(solution)/shard_map/all_to_all | solution.py:171
  455.3 3.4 convert_reduce_fusion
  458.7 2.3 gather_fusion.1
  461.1 1.5 broadcast_select_fusion
  462.6 1.6 reshape.215
  464.2 2.5 reduce_sum.386
  467.3 1.1 multiply_reduce_fusion
  468.4 0.8 fusion.74
  469.3 0.6 fusion.60
  469.9 1.5 collective-permute-start.2
  471.4 1.3 collective-permute-start.3
  472.7 0.7 fusion.54
  473.9 2.7 stack.134
  476.5 42.8 %all-reduce = (f32[1024]{0:T(1024)}, f32[1024,8]{0,1:T(8,128)}) all-reduce(f32[1024]{0:T(1024)S(1)} %get-tuple-element.8, f32[1024,8]{0,1:T(8,128)S(1)} %fusion.147), channel_id=1, replica_groups=mesh['seq'=32,'dp'=1] {'seq','dp'}, use_global_device_ids=true, to_apply=%region_44.46 | all-reduce | flops 9216 | bytes 73728 | tf_op jit(solution)/shard_map/psum | solution.py:189
  519.7 2.8 fusion.143
  522.4 79.1 %all-reduce.3.cloned.1.call-done = f32[31,1024]{1,0:T(8,128)} async-done(((f32[31,1024]{1,0:T(8,128)}), f32[31,1024]{1,0:T(8,128)}) %all-reduce.3.cloned.1.call-update) | async-done | bytes 126992 | tf_op jit(solution)/shard_map/psum | solution.py:189
  601.6 1.6 copy.37
  (208 shorter events, 6.3 us)
Async XLA Ops:
  7.2 129.3 %copy-start = (bf16[1,512,1024]{2,1,0:T(8,128)(2,1)S(1)}, bf16[1,512,1024]{2,1,0:T(8,128)(2,1)}, u32[]{:S(2)}) copy-start(bf16[1,512,1024]{2,1,0:T(8,128)(2,1)} %param.16) | copy-start | bytes 3145732
  8.1 8.7 %collective-permute-start = (bf16[15,1024]{1,0:T(8,128)(2,1)S(1)}, bf16[15,1024]{1,0:T(8,128)(2,1)S(1)}, u32[]{:S(2)}, u32[]{:S(2)}) collective-permute-start(bf16[15,1024]{1,0:T(8,128)(2,1)S(1)} %get-tuple-element.60), channel_id=1, source_target_pairs={{0,1},{1,2},{2,3},{3,4},{4,5},{5,6},{6,7},{7,8},{8,9},{9,10},{10,1... | collective-permute-start | bytes 92168 | tf_op jit(solution)/shard_map/ppermute | solution.py:16
  10.4 6.3 %collective-permute-start.1 = (bf16[15,1024]{1,0:T(8,128)(2,1)S(1)}, bf16[15,1024]{1,0:T(8,128)(2,1)S(1)}, u32[]{:S(2)}, u32[]{:S(2)}) collective-permute-start(bf16[15,1024]{1,0:T(8,128)(2,1)S(1)} %get-tuple-element.61), channel_id=1, source_target_pairs={{1,0},{2,1},{3,2},{4,3},{5,4},{6,5},{7,6},{8,7},{9,8},{10,9},{11,1... | collective-permute-start | bytes 92168 | tf_op jit(solution)/shard_map/ppermute | solution.py:17
  13.8 15.5 %copy-start.15 = (f32[1,1024]{1,0:T(1,128)}, f32[1,1024]{1,0:T(1,128)S(1)}, u32[]{:S(2)}) copy-start(f32[1,1024]{1,0:T(1,128)S(1)} %get-tuple-element.89) | copy-start | bytes 12292
  13.8 15.5 %copy-start.17 = (f32[1,1024]{1,0:T(1,128)}, f32[1,1024]{1,0:T(1,128)S(1)}, u32[]{:S(2)}) copy-start(f32[1,1024]{1,0:T(1,128)S(1)} %get-tuple-element.90) | copy-start | bytes 12292
  13.8 15.5 %copy-start.19 = (f32[1,1024]{1,0:T(1,128)}, f32[1,1024]{1,0:T(1,128)S(1)}, u32[]{:S(2)}) copy-start(f32[1,1024]{1,0:T(1,128)S(1)} %get-tuple-element.91) | copy-start | bytes 12292
  13.9 15.5 %copy-start.21 = (f32[1,1024]{1,0:T(1,128)}, f32[1,1024]{1,0:T(1,128)S(1)}, u32[]{:S(2)}) copy-start(f32[1,1024]{1,0:T(1,128)S(1)} %get-tuple-element.92) | copy-start | bytes 12292
  15.2 14.2 %copy-start.23 = (f32[1,1024]{1,0:T(1,128)}, f32[1,1024]{1,0:T(1,128)S(1)}, u32[]{:S(2)}) copy-start(f32[1,1024]{1,0:T(1,128)S(1)} %get-tuple-element.62) | copy-start | bytes 12292
  15.2 14.2 %copy-start.25 = (f32[1,1024]{1,0:T(1,128)}, f32[1,1024]{1,0:T(1,128)S(1)}, u32[]{:S(2)}) copy-start(f32[1,1024]{1,0:T(1,128)S(1)} %get-tuple-element.63) | copy-start | bytes 12292
  15.2 14.2 %copy-start.27 = (f32[1,1024]{1,0:T(1,128)}, f32[1,1024]{1,0:T(1,128)S(1)}, u32[]{:S(2)}) copy-start(f32[1,1024]{1,0:T(1,128)S(1)} %get-tuple-element.64) | copy-start | bytes 12292
  15.2 14.2 %copy-start.29 = (f32[1,1024]{1,0:T(1,128)}, f32[1,1024]{1,0:T(1,128)S(1)}, u32[]{:S(2)}) copy-start(f32[1,1024]{1,0:T(1,128)S(1)} %get-tuple-element.65) | copy-start | bytes 12292
  15.2 14.2 %copy-start.31 = (f32[1,1024]{1,0:T(1,128)}, f32[1,1024]{1,0:T(1,128)S(1)}, u32[]{:S(2)}) copy-start(f32[1,1024]{1,0:T(1,128)S(1)} %get-tuple-element.66) | copy-start | bytes 12292
  15.2 14.2 %copy-start.33 = (f32[1,1024]{1,0:T(1,128)}, f32[1,1024]{1,0:T(1,128)S(1)}, u32[]{:S(2)}) copy-start(f32[1,1024]{1,0:T(1,128)S(1)} %get-tuple-element.67) | copy-start | bytes 12292
  16.7 128.2 %copy-start.61 = (s32[256]{0:T(256)}, s32[256]{0:T(256)S(1)}, u32[]{:S(2)}) copy-start(s32[256]{0:T(256)S(1)} %get-tuple-element.49) | copy-start | bytes 3076
  29.4 104.7 %copy-start.83 = (bf16[1,1024,512]{2,1,0:T(8,128)(2,1)S(1)}, bf16[1,1024,512]{2,1,0:T(8,128)(2,1)}, u32[]{:S(2)}) copy-start(bf16[1,1024,512]{2,1,0:T(8,128)(2,1)} %param.15) | copy-start | bytes 3145732
  140.9 97.8 %all-to-all-start.1 = ((bf16[32,64,1024]{2,1,0:T(8,128)(2,1)}), bf16[32,64,1024]{2,1,0:T(8,128)(2,1)}, u32[]{:S(2)}, u32[]{:S(2)}) async-start(bf16[32,64,1024]{2,1,0:T(8,128)(2,1)} %bitcast.188), calls=%async_computation.1 | async-start | bytes 8388608 | tf_op jit(solution)/shard_map/all_to_all | solution.py:90
  145.0 99.2 %copy-start.63 = (s32[1024]{0:T(1024)}, s32[1024]{0:T(1024)S(1)}, u32[]{:S(2)}) copy-start(s32[1024]{0:T(1024)S(1)} %pad_clamp_fusion) | copy-start | bytes 12292
  145.0 99.1 %copy-start.64 = (s32[128]{0:T(128)}, s32[128]{0:T(128)S(1)}, u32[]{:S(2)}) copy-start(s32[128]{0:T(128)S(1)} %get-tuple-element.93) | copy-start | bytes 1540
  145.0 99.1 %copy-start.67 = (s32[128]{0:T(128)}, s32[128]{0:T(128)S(1)}, u32[]{:S(2)}) copy-start(s32[128]{0:T(128)S(1)} %get-tuple-element.94) | copy-start | bytes 1540
  252.5 97.3 %copy-start.86 = (f32[2048,512]{1,0:T(8,128)S(1)}, f32[2048,512]{1,0:T(8,128)}, u32[]{:S(2)}) copy-start(f32[2048,512]{1,0:T(8,128)} %copy-done.85) | copy-start | bytes 12582916
  357.6 97.7 %all-to-all-start.3 = ((bf16[32,64,1024]{2,1,0:T(8,128)(2,1)}), bf16[32,64,1024]{2,1,0:T(8,128)(2,1)}, u32[]{:S(2)}, u32[]{:S(2)}) async-start(bf16[32,64,1024]{2,1,0:T(8,128)(2,1)} %bitcast.187), calls=%async_computation.3 | async-start | bytes 8388608 | tf_op jit(solution)/shard_map/all_to_all | solution.py:171
  361.4 240.2 %all-reduce.3.cloned.1.call-start = ((), (), s32[]{:S(2)}) async-start(), calls=%async_computation.4 | async-start | bytes 262144 | tf_op jit(solution)/shard_map/psum | solution.py:189
  467.0 52.4 %copy-start.16 = (f32[1,1024]{1,0:T(1,128)S(1)}, f32[1,1024]{1,0:T(1,128)}, u32[]{:S(2)}) copy-start(f32[1,1024]{1,0:T(1,128)} %copy-done.15) | copy-start | bytes 12292
  467.1 52.4 %copy-start.18 = (f32[1,1024]{1,0:T(1,128)S(1)}, f32[1,1024]{1,0:T(1,128)}, u32[]{:S(2)}) copy-start(f32[1,1024]{1,0:T(1,128)} %copy-done.17) | copy-start | bytes 12292
  467.1 52.4 %copy-start.20 = (f32[1,1024]{1,0:T(1,128)S(1)}, f32[1,1024]{1,0:T(1,128)}, u32[]{:S(2)}) copy-start(f32[1,1024]{1,0:T(1,128)} %copy-done.19) | copy-start | bytes 12292
  467.1 52.4 %copy-start.22 = (f32[1,1024]{1,0:T(1,128)S(1)}, f32[1,1024]{1,0:T(1,128)}, u32[]{:S(2)}) copy-start(f32[1,1024]{1,0:T(1,128)} %copy-done.21) | copy-start | bytes 12292
  467.1 52.4 %copy-start.24 = (f32[1,1024]{1,0:T(1,128)S(1)}, f32[1,1024]{1,0:T(1,128)}, u32[]{:S(2)}) copy-start(f32[1,1024]{1,0:T(1,128)} %copy-done.23) | copy-start | bytes 12292
  467.1 52.4 %copy-start.26 = (f32[1,1024]{1,0:T(1,128)S(1)}, f32[1,1024]{1,0:T(1,128)}, u32[]{:S(2)}) copy-start(f32[1,1024]{1,0:T(1,128)} %copy-done.25) | copy-start | bytes 12292
  467.1 52.4 %copy-start.28 = (f32[1,1024]{1,0:T(1,128)S(1)}, f32[1,1024]{1,0:T(1,128)}, u32[]{:S(2)}) copy-start(f32[1,1024]{1,0:T(1,128)} %copy-done.27) | copy-start | bytes 12292
  467.1 52.4 %copy-start.30 = (f32[1,1024]{1,0:T(1,128)S(1)}, f32[1,1024]{1,0:T(1,128)}, u32[]{:S(2)}) copy-start(f32[1,1024]{1,0:T(1,128)} %copy-done.29) | copy-start | bytes 12292
  467.1 52.4 %copy-start.32 = (f32[1,1024]{1,0:T(1,128)S(1)}, f32[1,1024]{1,0:T(1,128)}, u32[]{:S(2)}) copy-start(f32[1,1024]{1,0:T(1,128)} %copy-done.31) | copy-start | bytes 12292
  467.1 52.4 %copy-start.34 = (f32[1,1024]{1,0:T(1,128)S(1)}, f32[1,1024]{1,0:T(1,128)}, u32[]{:S(2)}) copy-start(f32[1,1024]{1,0:T(1,128)} %copy-done.33) | copy-start | bytes 12292
  467.2 52.4 %copy-start.36 = (f32[1,1024]{1,0:T(1,128)S(1)}, f32[1,1024]{1,0:T(1,128)}, u32[]{:S(2)}) copy-start(f32[1,1024]{1,0:T(1,128)} %copy-done.35) | copy-start | bytes 12292
  467.2 52.4 %copy-start.38 = (f32[1,1024]{1,0:T(1,128)S(1)}, f32[1,1024]{1,0:T(1,128)}, u32[]{:S(2)}) copy-start(f32[1,1024]{1,0:T(1,128)} %copy-done.37) | copy-start | bytes 12292
  467.2 52.4 %copy-start.40 = (f32[1,1024]{1,0:T(1,128)S(1)}, f32[1,1024]{1,0:T(1,128)}, u32[]{:S(2)}) copy-start(f32[1,1024]{1,0:T(1,128)} %copy-done.39) | copy-start | bytes 12292
  467.2 52.4 %copy-start.42 = (f32[1,1024]{1,0:T(1,128)S(1)}, f32[1,1024]{1,0:T(1,128)}, u32[]{:S(2)}) copy-start(f32[1,1024]{1,0:T(1,128)} %copy-done.41) | copy-start | bytes 12292
  467.2 52.4 %copy-start.44 = (f32[1,1024]{1,0:T(1,128)S(1)}, f32[1,1024]{1,0:T(1,128)}, u32[]{:S(2)}) copy-start(f32[1,1024]{1,0:T(1,128)} %copy-done.43) | copy-start | bytes 12292
  467.2 52.4 %copy-start.46 = (f32[1,1024]{1,0:T(1,128)S(1)}, f32[1,1024]{1,0:T(1,128)}, u32[]{:S(2)}) copy-start(f32[1,1024]{1,0:T(1,128)} %copy-done.45) | copy-start | bytes 12292
  467.2 52.4 %copy-start.48 = (f32[1,1024]{1,0:T(1,128)S(1)}, f32[1,1024]{1,0:T(1,128)}, u32[]{:S(2)}) copy-start(f32[1,1024]{1,0:T(1,128)} %copy-done.47) | copy-start | bytes 12292
  467.2 52.4 %copy-start.50 = (f32[1,1024]{1,0:T(1,128)S(1)}, f32[1,1024]{1,0:T(1,128)}, u32[]{:S(2)}) copy-start(f32[1,1024]{1,0:T(1,128)} %copy-done.49) | copy-start | bytes 12292
  467.2 52.4 %copy-start.52 = (f32[1,1024]{1,0:T(1,128)S(1)}, f32[1,1024]{1,0:T(1,128)}, u32[]{:S(2)}) copy-start(f32[1,1024]{1,0:T(1,128)} %copy-done.51) | copy-start | bytes 12292
  467.2 52.4 %copy-start.54 = (f32[1,1024]{1,0:T(1,128)S(1)}, f32[1,1024]{1,0:T(1,128)}, u32[]{:S(2)}) copy-start(f32[1,1024]{1,0:T(1,128)} %copy-done.53) | copy-start | bytes 12292
  467.3 52.4 %copy-start.56 = (f32[1,1024]{1,0:T(1,128)S(1)}, f32[1,1024]{1,0:T(1,128)}, u32[]{:S(2)}) copy-start(f32[1,1024]{1,0:T(1,128)} %copy-done.55) | copy-start | bytes 12292
  467.3 52.4 %copy-start.58 = (f32[1,1024]{1,0:T(1,128)S(1)}, f32[1,1024]{1,0:T(1,128)}, u32[]{:S(2)}) copy-start(f32[1,1024]{1,0:T(1,128)} %copy-done.57) | copy-start | bytes 12292
  467.3 52.4 %copy-start.60 = (f32[1,1024]{1,0:T(1,128)S(1)}, f32[1,1024]{1,0:T(1,128)}, u32[]{:S(2)}) copy-start(f32[1,1024]{1,0:T(1,128)} %copy-done.59) | copy-start | bytes 12292
  469.9 49.5 %collective-permute-start.2 = (bf16[15,1024]{1,0:T(8,128)(2,1)S(1)}, bf16[15,1024]{1,0:T(8,128)(2,1)S(1)}, u32[]{:S(2)}, u32[]{:S(2)}) collective-permute-start(bf16[15,1024]{1,0:T(8,128)(2,1)S(1)} %get-tuple-element.56), channel_id=1, source_target_pairs={{0,1},{1,2},{2,3},{3,4},{4,5},{5,6},{6,7},{7,8},{8,9},{9,10},{10,1... | collective-permute-start | bytes 92168 | tf_op jit(solution)/shard_map/ppermute | solution.py:16
  471.4 48.0 %collective-permute-start.3 = (bf16[15,1024]{1,0:T(8,128)(2,1)S(1)}, bf16[15,1024]{1,0:T(8,128)(2,1)S(1)}, u32[]{:S(2)}, u32[]{:S(2)}) collective-permute-start(bf16[15,1024]{1,0:T(8,128)(2,1)S(1)} %get-tuple-element.57), channel_id=1, source_target_pairs={{1,0},{2,1},{3,2},{4,3},{5,4},{6,5},{7,6},{8,7},{9,8},{10,9},{11,1... | collective-permute-start | bytes 92168 | tf_op jit(solution)/shard_map/ppermute | solution.py:17
  519.7 83.5 %copy-start.1 = (bf16[1,512,1024]{2,1,0:T(8,128)(2,1)S(1)}, bf16[1,512,1024]{2,1,0:T(8,128)(2,1)}, u32[]{:S(2)}) copy-start(bf16[1,512,1024]{2,1,0:T(8,128)(2,1)} %param.16) | copy-start | bytes 3145732
  (47 other events, 298.9 us)
Sparse Core Ops, SparseCore 0:
  476.7 124.8 all-reduce.2
where the time goes:
time: 611 us; the launch traced here: 610 us
  waiting for transfers between devices  256 us (42%)
  blocking collectives  243 us (40%)
  other arithmetic  35.1 us (6%)
  matrix products  25.8 us (4%)
  local copies, waits for them, and re-layouts  19.8 us (3%)
  between operations  15.5 us (3%)
  starting transfers between devices  14.6 us (2%)
    all_to_all x1, blocking collectives, body(): lax.all_to_all(spread(repeated), 'seq', split_axis=0, concat_axis=0, tile...  103 us
    all_to_all x1, blocking collectives, body(): lax.all_to_all(spread(grad_values), 'seq', split_axis=0, concat_axis=0, t...  97.3 us
    all_to_all x1, waiting for transfers between devices, combine_back(): lax.all_to_all(partial_rows, 'seq', split_axis=0, concat_axis=0, tiled=True)  93.5 us
    all_to_all x1, waiting for transfers between devices, body(): lax.all_to_all(grad_part.reshape(arrived.shape), 'seq', split_axis=0, con...  83.7 us
    psum x1, waiting for transfers between devices, body(): lax.psum((kernel_term, gain_term, router_term), ('seq', 'dp'))  79.1 us
    psum x1, blocking collectives, body(): lax.psum((kernel_term, gain_term, router_term), ('seq', 'dp'))  42.8 us
  transfers between devices with their start and end apart: 7, of which 3 were waited for; matrix products, arithmetic and copies ran while one was open for 4% of the time, Pallas kernels for 0%

commit v1 on v0

--- a/solution.py
+++ b/solution.py
@@ -1,7 +1,11 @@
 import jax
 import jax.numpy as jnp
 from jax import lax
+from jax.experimental import pallas as pl
+from jax.experimental.pallas import tpu as pltpu
 from jax.sharding import PartitionSpec as P
+
+MESH = pl.DeviceIdType.MESH
 
 eps = 1e-06
 
@@ -86,8 +90,272 @@
     return (router_term, normed_term)
 
 
-def combine_back(partial_rows):
-    return lax.all_to_all(partial_rows, "seq", split_axis=0, concat_axis=0, tiled=True)
+def dot_over(left, right, left_dim, right_dim):
+    return lax.dot_general(
+        left, right, (((left_dim,), (right_dim,)), ((), ())), preferred_element_type=jnp.float32
+    )
+
+
+def moe_kernel(
+    packed, w_in, w_out, back, grad_in, grad_out,
+    rows, part, core_got, x_send, x_got, kept, final, sems,
+):
+    count, cap, width = packed.shape
+    depth = width // 2
+    me = lax.axis_index("seq")
+    e, x, c = me // 4, (me % 4) // 2, me % 2
+    own = c * 2 + x
+    own_x = c * 2 + 1 - x
+    other = (1 - c) * 2 + x
+    other_x = (1 - c) * 2 + 1 - x
+
+    def place(e_to, x_to, c_to):
+        return {"seq": e_to * 4 + x_to * 2 + c_to}
+
+    core_peer, x_peer = place(e, x, 1 - c), place(e, 1 - x, c)
+
+    def copy(kind, k, source, target, device):
+        return pltpu.make_async_remote_copy(
+            src_ref=source,
+            dst_ref=target,
+            send_sem=sems.at[0, kind, k],
+            recv_sem=sems.at[1, kind, k],
+            device_id=device,
+            device_id_type=MESH,
+        )
+
+    def block(k):
+        return (e + count - k) % count
+
+    def dispatch(k):
+        to = (e + k) % count
+        return copy(0, k, packed.at[to], rows.at[e, own], place(to, x, c))
+
+    def near(kind, k, section, device):
+        piece = rows.at[block(k), section]
+        return copy(kind, k, piece, piece, device)
+
+    def core_sum(k):
+        f = block(k)
+        return copy(4, k, part.at[f, pl.ds((1 - c) * 2, 2)], core_got.at[f], core_peer)
+
+    def x_sum(k):
+        f = block(k)
+        return copy(5, k, x_send.at[f], x_got.at[f], x_peer)
+
+    def give_back(k, slot):
+        f = block(k)
+        return copy(6, k, final.at[f], back.at[slot], place(f, x, c))
+
+    barrier = pltpu.get_barrier_semaphore()
+    pl.semaphore_signal(barrier, inc=1, device_id=core_peer, device_id_type=MESH)
+    pl.semaphore_signal(barrier, inc=1, device_id=x_peer, device_id_type=MESH)
+
+    def greet(k, carry):
+        pl.semaphore_signal(
+            barrier, inc=1, device_id=place((e + k) % count, x, c), device_id_type=MESH
+        )
+        return carry
+
+    lax.fori_loop(1, count, greet, 0)
+    pl.semaphore_wait(barrier, count + 1)
+
+    def send_first(k, carry):
+        dispatch(k).start()
+        return carry
+
+    lax.fori_loop(1, count, send_first, 0)
+    rows[e, own] = packed[e]
+    grad_in[...] = jnp.zeros_like(grad_in)
+    grad_out[...] = jnp.zeros_like(grad_out)
+
+    def stage_spread(k):
+        f = block(k)
+
+        @pl.when(k > 0)
+        def _():
+            copy(0, k, packed.at[f], rows.at[f, own], place(f, x, c)).wait_recv()
+
+        near(1, k, own, x_peer).start()
+        near(2, k, own, core_peer).start()
+
+    def stage_forward(k):
+        near(1, k, own_x, x_peer).wait_recv()
+        near(3, k, own_x, core_peer).start()
+
+    def stage_compute(k):
+        f = block(k)
+        near(2, k, other, core_peer).wait_recv()
+        near(3, k, other_x, core_peer).wait_recv()
+        values = rows[f].reshape(4 * cap, width)
+        normed, grads = values[:, :depth], values[:, depth:]
+        pre_act = dot_over(normed, w_in[...], 1, 0)
+        hidden_f, slope = swish_parts(pre_act)
+        hidden = hidden_f.astype(jnp.bfloat16)
+        grad_pre = (dot_over(grads, w_out[...], 1, 1) * slope).astype(jnp.bfloat16)
+        part[f, :, :, :depth] = (
+            dot_over(hidden, w_out[...], 1, 0).astype(jnp.bfloat16).reshape(4, cap, depth)
+        )
+        part[f, :, :, depth:] = (
+            dot_over(grad_pre, w_in[...], 1, 1).astype(jnp.bfloat16).reshape(4, cap, depth)
+        )
+        core_sum(k).start()
+        grad_out[...] += dot_over(hidden, grads, 0, 0)
+        grad_in[...] += dot_over(normed, grad_pre, 0, 0)
+
+    def stage_core(k):
+        f = block(k)
+        core_sum(k).wait_recv()
+        x_send[f] = (
+            part[f, own_x].astype(jnp.float32) + core_got[f, 1 - x].astype(jnp.float32)
+        ).astype(jnp.bfloat16)
+        x_sum(k).start()
+        kept[f] = part[f, own].astype(jnp.float32) + core_got[f, x].astype(jnp.float32)
+
+    def stage_back(k):
+        f = block(k)
+        x_sum(k).wait_recv()
+        total = (kept[f] + x_got[f].astype(jnp.float32)).astype(jnp.bfloat16)
+
+        @pl.when(k == 0)
+        def _():
+            back[e] = total
+
+        @pl.when(k > 0)
+        def _():
+            final[f] = total
+            give_back(k, e).start()
+
+    stages = (stage_back, stage_core, stage_compute, stage_forward, stage_spread)
+
+    def step(t, carry):
+        for lag, stage in zip((4, 3, 2, 1, 0), stages):
+            k = t - lag
+
+            @pl.when((k >= 0) & (k < count))
+            def _(stage=stage, k=k):
+                stage(k)
+
+        return carry
+
+    lax.fori_loop(0, count + 4, step, 0)
+
+    def finish(k, carry):
+        @pl.when(k > 0)
+        def _():
+            dispatch(k).wait_send()
+            give_back(k, e).wait_send()
+            give_back(k, (e + k) % count).wait_recv()
+
+        near(1, k, own, x_peer).wait_send()
+        near(2, k, own, core_peer).wait_send()
+        near(3, k, own_x, core_peer).wait_send()
+        core_sum(k).wait_send()
+        x_sum(k).wait_send()
+        return carry
+
+    lax.fori_loop(0, count, finish, 0)
+
+
+def moe(packed, w_in, w_out):
+    count, cap, width = packed.shape
+    vmem = pl.BlockSpec(memory_space=pltpu.VMEM)
+    half = jnp.bfloat16
+    return pl.pallas_call(
+        moe_kernel,
+        out_shape=(
+            jax.ShapeDtypeStruct(packed.shape, half),
+            jax.ShapeDtypeStruct(w_in.shape, jnp.float32),
+            jax.ShapeDtypeStruct(w_out.shape, jnp.float32),
+        ),
+        in_specs=[vmem] * 3,
+        out_specs=(vmem,) * 3,
+        scratch_shapes=[
+            pltpu.VMEM((count, 4, cap, width), half),
+            pltpu.VMEM((count, 4, cap, width), half),
+            pltpu.VMEM((count, 2, cap, width), half),
+            pltpu.VMEM((count, cap, width), half),
+            pltpu.VMEM((count, cap, width), half),
+            pltpu.VMEM((count, cap, width), jnp.float32),
+            pltpu.VMEM((count, cap, width), half),
+            pltpu.SemaphoreType.DMA((2, 7, count)),
+        ],
+        compiler_params=pltpu.CompilerParams(
+            collective_id=0, has_side_effects=True, vmem_limit_bytes=56 * 2**20
+        ),
+    )(packed, w_in, w_out)
+
+
+def sum_kernel(terms, totals, got, sems):
+    count = terms.shape[0]
+    seq_size = lax.axis_size("seq")
+    me = lax.axis_index("dp") * seq_size + lax.axis_index("seq")
+
+    def place(number):
+        return {"dp": number // seq_size, "seq": number % seq_size}
+
+    def copy(phase, j, source, target, number):
+        return pltpu.make_async_remote_copy(
+            src_ref=source,
+            dst_ref=target,
+            send_sem=sems.at[phase, 0, j],
+            recv_sem=sems.at[phase, 1, j],
+            device_id=place(number),
+            device_id_type=MESH,
+        )
+
+    def ahead(j):
+        return (me + j) % count
+
+    def behind(j):
+        return (me + count - j) % count
+
+    def every(action):
+        def one(j, carry):
+            action(j)
+            return carry
+
+        lax.fori_loop(1, count, one, 0)
+
+    barrier = pltpu.get_barrier_semaphore()
+    every(
+        lambda j: pl.semaphore_signal(
+            barrier, inc=1, device_id=place(ahead(j)), device_id_type=MESH
+        )
+    )
+    pl.semaphore_wait(barrier, count - 1)
+    every(lambda j: copy(0, j, terms.at[ahead(j)], got.at[me], ahead(j)).start())
+    got[me] = terms[me]
+    every(lambda j: copy(0, j, terms.at[ahead(j)], got.at[behind(j)], ahead(j)).wait_recv())
+    totals[me] = jnp.sum(got[...], axis=0)
+    every(lambda j: copy(1, j, totals.at[me], totals.at[me], ahead(j)).start())
+    every(lambda j: copy(1, j, totals.at[me], totals.at[behind(j)], ahead(j)).wait_recv())
+    every(lambda j: copy(0, j, terms.at[ahead(j)], got.at[me], ahead(j)).wait_send())
+    every(lambda j: copy(1, j, totals.at[me], totals.at[me], ahead(j)).wait_send())
+
+
+def sum_everywhere(values):
+    count = lax.axis_size("seq") * lax.axis_size("dp")
+    flat = jnp.concatenate([value.reshape(-1) for value in values])
+    tall = -(-flat.shape[0] // (count * 1024)) * 8
+    padded = jnp.pad(flat, (0, count * tall * 128 - flat.shape[0])).reshape(count, tall, 128)
+    vmem = pl.BlockSpec(memory_space=pltpu.VMEM)
+    totals = pl.pallas_call(
+        sum_kernel,
+        out_shape=jax.ShapeDtypeStruct(padded.shape, jnp.float32),
+        in_specs=[vmem],
+        out_specs=vmem,
+        scratch_shapes=[
+            pltpu.VMEM(padded.shape, jnp.float32),
+            pltpu.SemaphoreType.DMA((2, 2, count)),
+        ],
+        compiler_params=pltpu.CompilerParams(collective_id=1, has_side_effects=True),
+    )(padded).reshape(-1)
+    results, start = [], 0
+    for value in values:
+        results.append(totals[start : start + value.size].reshape(value.shape))
+        start += value.size
+    return results
 
 
 def body(frames, kernel, norm_gain, router, experts, w_in, w_out, cotangent):
@@ -99,7 +367,6 @@
     expert_count = router.shape[1]
     top_count = experts.shape[2]
     capacity = 2 * row_count * top_count // expert_count
-    group_size = lax.axis_size("seq") // expert_count
     in_weights = w_in[0]
     out_weights = w_out[0]
     padded = padded_2(inputs_dev, (("seq", 0),), half_width)
@@ -122,57 +389,25 @@
             jnp.bfloat16
         )
 
-    def spread(values):
-        return jnp.repeat(pack(values).reshape(expert_count, capacity, width), group_size, axis=0)
-
-    def slice_totals(returned):
-        totals = jnp.sum(
-            returned.astype(jnp.float32).reshape(expert_count, group_size, capacity, width), axis=1
-        )
-        return totals.reshape(expert_count * capacity, width)
-
-    def gather_back(totals):
-        picked = jnp.take(totals, position, axis=0)
-        return picked.reshape(row_count, top_count, width)
-
     repeated = jnp.repeat(normed_b, top_count, axis=0)
     upstream = cotangent[0].astype(jnp.float32)
     grad_assigned = jnp.stack([gate_one[:, None] * upstream, gate_two[:, None] * upstream], axis=1)
     grad_values = grad_assigned.reshape(row_count * top_count, width).astype(jnp.bfloat16)
-    arrived = lax.all_to_all(spread(repeated), "seq", split_axis=0, concat_axis=0, tiled=True)
-    flat_rows = arrived.reshape(-1, width)
-    pre_act = jnp.dot(flat_rows, in_weights, preferred_element_type=jnp.float32)
-    hidden = swish_parts(pre_act)[0].astype(jnp.bfloat16)
-    partial_rows = jnp.dot(hidden, out_weights, preferred_element_type=jnp.float32).astype(
-        jnp.bfloat16
-    )
-    results = (combine_back(partial_rows.reshape(arrived.shape)), arrived)
-    arrived = results[1]
-    assigned = gather_back(slice_totals(results[0]))
+    packed = pack(jnp.concatenate([repeated, grad_values], axis=1))
+    back, in_term, out_term = moe(
+        packed.reshape(expert_count, capacity, 2 * width), in_weights, out_weights
+    )
+    back = back.reshape(expert_count * capacity, 2 * width)
+    assigned = dot_over(dispatch_table, back[:, :width], 0, 0).reshape(
+        row_count, top_count, width
+    )
     out_one = assigned[:, 0]
     out_two = assigned[:, 1]
     mixed = (summed + gate_one[:, None] * out_one + gate_two[:, None] * out_two).astype(
         jnp.bfloat16
     )
-    incoming = lax.all_to_all(spread(grad_values), "seq", split_axis=0, concat_axis=0, tiled=True)
-    flat_rows = arrived.reshape(-1, width)
-    flat_grads = incoming.reshape(-1, width)
-    pre_act = jnp.dot(flat_rows, in_weights, preferred_element_type=jnp.float32)
-    hidden_f, slope = swish_parts(pre_act)
-    hidden = hidden_f.astype(jnp.bfloat16)
-    grad_hidden = jnp.dot(flat_grads, out_weights.T, preferred_element_type=jnp.float32)
-    grad_pre = (grad_hidden * slope).astype(jnp.bfloat16)
-    out_term = jnp.dot(hidden.T, flat_grads, preferred_element_type=jnp.float32)
-    in_term = jnp.dot(flat_rows.T, grad_pre, preferred_element_type=jnp.float32)
-    grad_part = jnp.dot(grad_pre, in_weights.T, preferred_element_type=jnp.float32).astype(
-        jnp.bfloat16
-    )
-    grad_totals = slice_totals(
-        lax.all_to_all(
-            grad_part.reshape(arrived.shape), "seq", split_axis=0, concat_axis=0, tiled=True
-        )
-    )
-    normed_grads = jnp.sum(gather_back(grad_totals), axis=1)
+    both = jnp.sum(dispatch_table.reshape(-1, row_count, top_count), axis=2)
+    normed_grads = dot_over(both, back[:, width:], 0, 0)
     router_term, normed_term = gate_backward(
         upstream, out_one, out_two, gate_one, gate_two, pick_diff, normed_b, router
     )
@@ -186,13 +421,13 @@
         jnp.bfloat16
     )
     kernel_term = kernel_terms(padded, upstream_total, length, row_count)
-    grad_kernel, grad_gain, grad_router = lax.psum(
-        (kernel_term, gain_term, router_term), ("seq", "dp")
-    )
-    grad_in, grad_out = (
-        lax.psum(in_term.astype(jnp.bfloat16), "dp").astype(jnp.float32),
-        lax.psum(out_term.astype(jnp.bfloat16), "dp").astype(jnp.float32),
-    )
+    grad_kernel, grad_gain, grad_router = sum_everywhere((kernel_term, gain_term, router_term))
+    grad_in, grad_out = in_term, out_term
+    if lax.axis_size("dp") > 1:
+        grad_in, grad_out = (
+            lax.psum(in_term.astype(jnp.bfloat16), "dp").astype(jnp.float32),
+            lax.psum(out_term.astype(jnp.bfloat16), "dp").astype(jnp.float32),
+        )
     return (
         mixed[None],
         grad_frames[None],

time: 611 us -> 204 us (0.33)
  waiting for transfers between devices: 256 us -> 0.01 us
  blocking collectives: 243 us -> 0 us
  Pallas kernels: 0 us -> 157 us
  matrix products: 25.8 us -> 4.9 us
  other arithmetic: 35.1 us -> 19.9 us
  between operations: 15.5 us -> 1.01 us
  starting transfers between devices: 14.6 us -> 6.23 us
    all_to_all x2 -> x0, blocking collectives: 200 us -> none  [the longest x1 103 us: body(): lax.all_to_all(spread(repeated), 'seq', split_axis=0, concat_axis=0, tile...]
    all_to_all x2 -> x0, waiting for transfers between devices: 177 us -> none  [the longest x1 93.5 us: combine_back(): lax.all_to_all(partial_rows, 'seq', split_axis=0, concat_axis=0, tiled=True)]
    pallas_call x0 -> x2, Pallas kernels: none -> 157 us  [the longest x1 133 us: moe(): pl.pallas_call(moe_kernel, out_shape=(jax.ShapeDtypeStruct(packed.shape,...]
    psum x1 -> x0, waiting for transfers between devices: 79.1 us -> none  [body(): lax.psum((kernel_term, gain_term, router_term), ('seq', 'dp'))]
    psum x1 -> x0, blocking collectives: 42.8 us -> none  [body(): lax.psum((kernel_term, gain_term, router_term), ('seq', 'dp'))]
    dot_general x6 -> x2, matrix products: 24.3 us -> 2.17 us  [dot_over(): lax.dot_general(left, right, (((left_dim,), (right_dim,)), ((), ())), pre...]
    reduce_sum x4 -> x1, other arithmetic: 10.3 us -> 0.08 us  [body(): both = jnp.sum(dispatch_table.reshape(-1, row_count, top_count), axis=2)]
    all_to_all x2 -> x0, starting transfers between devices: 7.86 us -> none  [the longest x1 4.02 us: combine_back(): lax.all_to_all(partial_rows, 'seq', split_axis=0, concat_axis=0, tiled=True)]
  transfers between devices with their start and end apart: 7 -> 4, of which waited for: 3 -> 0; matrix products, arithmetic and copies ran while one was open for 4% -> 5% of each run, Pallas kernels for 0% -> 12%
where the time goes in v1:
time: 204 us
  Pallas kernels  157 us (77%)
  other arithmetic  19.9 us (10%)
  local copies, waits for them, and re-layouts  14.2 us (7%)
  starting transfers between devices  6.23 us (3%)
  matrix products  4.9 us (2%)
    pallas_call x1, Pallas kernels, moe(): pl.pallas_call(moe_kernel, out_shape=(jax.ShapeDtypeStruct(packed.shape,...  133 us
    pallas_call x1, Pallas kernels, sum_everywhere(): pl.pallas_call(sum_kernel, out_shape=jax.ShapeDtypeStruct(padded.shape, j...  24.2 us
    reduce_sum x1, other arithmetic, normalize(): square = jnp.mean(summed * summed, axis=-1, keepdims=True)  9.39 us
    unnamed x18, local copies, waits for them, and re-layouts  5.38 us
  transfers between devices with their start and end apart: 4, of which 0 were waited for; matrix products, arithmetic and copies ran while one was open for 5% of the time, Pallas kernels for 12%

profile of v1, /device:TPU:0, one launch (start us, length us, event | category | flops | bytes accessed | tf_op | source)
XLA Modules:
  0.0 203.5 jit_solution(15899188373373020104)
XLA Ops:
  0.7 0.8 slice_bitcast_fusion.1
  1.5 2.4 %collective-permute-start = (bf16[15,1024]{1,0:T(8,128)(2,1)S(1)}, bf16[15,1024]{1,0:T(8,128)(2,1)S(1)}, u32[]{:S(2)}, u32[]{:S(2)}) collective-permute-start(bf16[15,1024]{1,0:T(8,128)(2,1)S(1)} %get-tuple-element.91), channel_id=1, source_target_pairs={{0,1},{1,2},{2,3},{3,4},{4,5},{5,6},{6,7},{7,8},{8,9},{9,10},{10,1... | collective-permute-start | bytes 92168 | tf_op jit(solution)/shard_map/ppermute | solution.py:20
  3.9 1.3 collective-permute-start.1
  5.2 1.2 slice_convert_fusion.30
  6.4 1.0 slice_convert_fusion.29
  7.4 0.8 copy.35
  8.2 0.1 eq.77
  8.3 0.1 reshape_squeeze.3
  8.5 0.6 reduce-window.6
  9.1 0.2 slice_reduce_fusion.2
  9.4 0.1 reduce_sum.371
  9.7 0.2 slice_reduce_fusion.1
  9.9 9.4 %multiply_reduce_fusion.2 = (f32[128]{0:T(128)S(1)}, f32[128,1024]{1,0:T(8,128)S(1)}) fusion(bf16[15,1024]{1,0:T(8,128)(2,1)S(1)} %collective-permute-done.1, bf16[128,1024]{1,0:T(8,128)(2,1)} %bitcast.135, f32[1024]{0:T(1024)S(1)} %bitcast.207, f32[1024]{0:T(1024)S(1)} %bitcast.209, f32[1024]{0:T(1024)S(1)} %bitcast.151, f32[1024]{0:T(1024)S(1)} %bitcast.153, ...), kind=kLoop, calls=%fused_computation.246 | loop fusion | flops 24248192 | bytes 975360 | tf_op jit(solution)/shard_map/reduce_sum | solution.py:54
  19.5 0.2 fusion
  19.7 0.2 fusion.72
  19.9 0.5 copy.38
  20.5 0.2 convert_element_type.324
  20.7 0.3 broadcast_in_dim.12
  21.0 0.2 reshape.183
  21.2 2.0 %convolution_convert_fusion = bf16[512,2048]{1,0:T(8,128)(2,1)} fusion(bf16[256,1024]{1,0:T(8,128)(2,1)S(1)} %convert_element_type.324, bf16[256,1024]{1,0:T(8,128)(2,1)S(1)} %reshape.183, s32[256]{0:T(256)S(1)} %multiply_add_fusion.1), kind=kOutput, calls=%fused_computation | convolution fusion | flops 540147712 | bytes 3146752 | tf_op jit(solution)/shard_map/dot_general | solution.py:388
  23.2 133.0 %shard_map.135 = (bf16[8,64,2048]{2,1,0:T(8,128)(2,1)}, f32[1024,512]{1,0:T(8,128)}, f32[512,1024]{1,0:T(8,128)}) custom-call(bf16[8,64,2048]{2,1,0:T(8,128)(2,1)} %bitcast.134, bf16[1024,512]{1,0:T(8,128)(2,1)} %bitcast.147, bf16[512,1024]{1,0:T(8,128)(2,1)} %bitcast.148), custom_call_target="tpu_custom_call" | custom-call | tf_op jit(solution)/shard_map/pallas_call | solution.py:264
  156.2 1.7 fusion.2
  158.0 0.6 reshape.186
  158.6 0.8 fusion.157
  159.4 1.0 fusion.75
  160.5 0.3 fusion.147
  160.7 0.3 fusion.146
  161.1 0.5 multiply_reduce_fusion
  161.6 0.8 fusion.71
  162.4 0.6 fusion.57
  163.0 0.7 fusion.51
  163.7 0.5 fusion.42
  164.1 0.2 stack.134
  164.4 0.3 reshape.188
  164.7 1.3 collective-permute-start.2
  166.0 1.3 collective-permute-start.3
  167.3 0.7 select_maximum_fusion
  168.0 24.2 %shard_map.136 = f32[32,16,128]{2,1,0:T(8,128)} custom-call(f32[32,16,128]{2,1,0:T(8,128)} %bitcast.146), custom_call_target="tpu_custom_call" | custom-call | tf_op jit(solution)/shard_map/pallas_call | solution.py:343
  192.2 0.8 slice.531
  193.0 1.0 slice.528
  194.0 0.3 reshape.191
  194.3 0.8 copy.43
  195.0 0.7 slice.628
  195.7 1.3 slice.629
  197.1 2.8 %fusion.142 = bf16[1,128,1024]{2,1,0:T(8,128)(2,1)} fusion(f32[128,1024]{1,0:T(8,128)S(1)} %get-tuple-element.78, f32[158,1024]{1,0:T(8,128)S(1)} %maximum_convert_fusion, f32[1024]{0:T(1024)S(1)} %bitcast.208, f32[1024]{0:T(1024)S(1)} %bitcast.210, f32[1024]{0:T(1024)S(1)} %bitcast.152, f32[1024]{0:T(1024)S(1)} %bitcast.154, f32[1024]{0:T(1024)S(1)} %bitcast.156, ...), kind=kLoop, calls=%fused_computation.286 | loop fusion | flops 8257536 | bytes 17166336 | tf_op jit(solution)/shard_map/broadcast_in_dim | solution.py:433
  199.8 1.3 copy.63
  201.2 1.0 copy-done.4
  202.2 1.3 copy.64
  (34 shorter events, 0.8 us)
Async XLA Ops:
  0.6 18.8 %copy-start = (bf16[1024,8]{0,1:T(8,128)(2,1)S(1)}, bf16[1024,8]{0,1:T(8,128)(2,1)}, u32[]{:S(2)}) copy-start(bf16[1024,8]{0,1:T(8,128)(2,1)} %param.11) | copy-start | bytes 49156
  0.6 18.7 %copy-start.6 = (f32[1024]{0:T(1024)S(1)}, f32[1024]{0:T(1024)}, u32[]{:S(2)}) copy-start(f32[1024]{0:T(1024)} %param.10) | copy-start | bytes 12292
  0.7 19.0 %copy-start.2 = (bf16[1,128,1024]{2,1,0:T(8,128)(2,1)S(1)}, bf16[1,128,1024]{2,1,0:T(8,128)(2,1)}, u32[]{:S(2)}) copy-start(bf16[1,128,1024]{2,1,0:T(8,128)(2,1)} %param.15) | copy-start | bytes 786436
  1.5 8.4 %collective-permute-start = (bf16[15,1024]{1,0:T(8,128)(2,1)S(1)}, bf16[15,1024]{1,0:T(8,128)(2,1)S(1)}, u32[]{:S(2)}, u32[]{:S(2)}) collective-permute-start(bf16[15,1024]{1,0:T(8,128)(2,1)S(1)} %get-tuple-element.91), channel_id=1, source_target_pairs={{0,1},{1,2},{2,3},{3,4},{4,5},{5,6},{6,7},{7,8},{8,9},{9,10},{10,1... | collective-permute-start | bytes 92168 | tf_op jit(solution)/shard_map/ppermute | solution.py:20
  3.9 6.1 %collective-permute-start.1 = (bf16[15,1024]{1,0:T(8,128)(2,1)S(1)}, bf16[15,1024]{1,0:T(8,128)(2,1)S(1)}, u32[]{:S(2)}, u32[]{:S(2)}) collective-permute-start(bf16[15,1024]{1,0:T(8,128)(2,1)S(1)} %get-tuple-element.92), channel_id=1, source_target_pairs={{1,0},{2,1},{3,2},{4,3},{5,4},{6,5},{7,6},{8,7},{9,8},{10,9},{11,1... | collective-permute-start | bytes 92168 | tf_op jit(solution)/shard_map/ppermute | solution.py:21
  159.4 1.7 copy-start.3
  160.4 1.1 copy-start.1
  164.7 32.3 %collective-permute-start.2 = (bf16[15,1024]{1,0:T(8,128)(2,1)S(1)}, bf16[15,1024]{1,0:T(8,128)(2,1)S(1)}, u32[]{:S(2)}, u32[]{:S(2)}) collective-permute-start(bf16[15,1024]{1,0:T(8,128)(2,1)S(1)} %get-tuple-element.87), channel_id=1, source_target_pairs={{0,1},{1,2},{2,3},{3,4},{4,5},{5,6},{6,7},{7,8},{8,9},{9,10},{10,1... | collective-permute-start | bytes 92168 | tf_op jit(solution)/shard_map/ppermute | solution.py:20
  166.0 31.0 %collective-permute-start.3 = (bf16[15,1024]{1,0:T(8,128)(2,1)S(1)}, bf16[15,1024]{1,0:T(8,128)(2,1)S(1)}, u32[]{:S(2)}, u32[]{:S(2)}) collective-permute-start(bf16[15,1024]{1,0:T(8,128)(2,1)S(1)} %get-tuple-element.88), channel_id=1, source_target_pairs={{1,0},{2,1},{3,2},{4,3},{5,4},{6,5},{7,6},{8,7},{9,8},{10,9},{11,1... | collective-permute-start | bytes 92168 | tf_op jit(solution)/shard_map/ppermute | solution.py:21
  197.1 2.8 %copy-start.5 = (f32[1024,512]{1,0:T(8,128)S(1)}, f32[1024,512]{1,0:T(8,128)}, u32[]{:S(2)}) copy-start(f32[1024,512]{1,0:T(8,128)} %get-tuple-element.11) | copy-start | bytes 6291460
  199.8 2.3 %copy-start.4 = (f32[512,1024]{1,0:T(8,128)S(1)}, f32[512,1024]{1,0:T(8,128)}, u32[]{:S(2)}) copy-start(f32[512,1024]{1,0:T(8,128)} %get-tuple-element.12) | copy-start | bytes 6291460

commit v2 on v1

--- a/solution.py
+++ b/solution.py
@@ -226,10 +226,16 @@
             final[f] = total
             give_back(k, e).start()
 
-    stages = (stage_back, stage_core, stage_compute, stage_forward, stage_spread)
+    stages = (
+        (4, stage_back),
+        (3, stage_core),
+        (1, stage_forward),
+        (0, stage_spread),
+        (2, stage_compute),
+    )
 
     def step(t, carry):
-        for lag, stage in zip((4, 3, 2, 1, 0), stages):
+        for lag, stage in stages:
             k = t - lag
 
             @pl.when((k >= 0) & (k < count))
@@ -286,59 +292,87 @@
     )(packed, w_in, w_out)
 
 
-def sum_kernel(terms, totals, got, sems):
-    count = terms.shape[0]
+def sum_kernel(terms, totals, near_got, near_sum, far_got, sems):
     seq_size = lax.axis_size("seq")
-    me = lax.axis_index("dp") * seq_size + lax.axis_index("seq")
-
-    def place(number):
+    seq, dp = lax.axis_index("seq"), lax.axis_index("dp")
+    groups = terms.shape[1]
+    m, h = seq % 4, dp * (seq_size // 4) + seq // 4
+
+    def mate(j):
+        return {"dp": dp, "seq": seq // 4 * 4 + (m + j) % 4}
+
+    def peer(j):
+        number = (h + j) % groups * 4 + m
         return {"dp": number // seq_size, "seq": number % seq_size}
 
-    def copy(phase, j, source, target, number):
+    def copy(phase, j, source, target, device):
         return pltpu.make_async_remote_copy(
             src_ref=source,
             dst_ref=target,
             send_sem=sems.at[phase, 0, j],
             recv_sem=sems.at[phase, 1, j],
-            device_id=place(number),
+            device_id=device,
             device_id_type=MESH,
         )
 
-    def ahead(j):
-        return (me + j) % count
-
-    def behind(j):
-        return (me + count - j) % count
-
-    def every(action):
+    def every(size, action):
         def one(j, carry):
             action(j)
             return carry
 
-        lax.fori_loop(1, count, one, 0)
+        lax.fori_loop(1, size, one, 0)
+
+    def behind_m(j):
+        return (m + 4 - j) % 4
+
+    def behind_h(j):
+        return (h + groups - j) % groups
+
+    def near_in(j, slot):
+        return copy(0, j, terms.at[(m + j) % 4], near_got.at[slot], mate(j))
+
+    def far_in(j, slot):
+        return copy(1, j, near_sum.at[(h + j) % groups], far_got.at[slot], peer(j))
+
+    def far_out(j, slot):
+        return copy(2, j, totals.at[m, h], totals.at[m, slot], peer(j))
+
+    def near_out(j, slot):
+        return copy(3, j, totals.at[m], totals.at[slot], mate(j))
 
     barrier = pltpu.get_barrier_semaphore()
-    every(
-        lambda j: pl.semaphore_signal(
-            barrier, inc=1, device_id=place(ahead(j)), device_id_type=MESH
-        )
-    )
-    pl.semaphore_wait(barrier, count - 1)
-    every(lambda j: copy(0, j, terms.at[ahead(j)], got.at[me], ahead(j)).start())
-    got[me] = terms[me]
-    every(lambda j: copy(0, j, terms.at[ahead(j)], got.at[behind(j)], ahead(j)).wait_recv())
-    totals[me] = jnp.sum(got[...], axis=0)
-    every(lambda j: copy(1, j, totals.at[me], totals.at[me], ahead(j)).start())
-    every(lambda j: copy(1, j, totals.at[me], totals.at[behind(j)], ahead(j)).wait_recv())
-    every(lambda j: copy(0, j, terms.at[ahead(j)], got.at[me], ahead(j)).wait_send())
-    every(lambda j: copy(1, j, totals.at[me], totals.at[me], ahead(j)).wait_send())
-
-
-def sum_everywhere(values):
-    count = lax.axis_size("seq") * lax.axis_size("dp")
-    flat = jnp.concatenate([value.reshape(-1) for value in values])
-    tall = -(-flat.shape[0] // (count * 1024)) * 8
-    padded = jnp.pad(flat, (0, count * tall * 128 - flat.shape[0])).reshape(count, tall, 128)
+
+    def greet(device):
+        pl.semaphore_signal(barrier, inc=1, device_id=device, device_id_type=MESH)
+
+    every(4, lambda j: greet(mate(j)))
+    every(groups, lambda j: greet(peer(j)))
+    pl.semaphore_wait(barrier, groups + 2)
+    every(4, lambda j: near_in(j, m).start())
+    near_got[m] = terms[m]
+    every(4, lambda j: near_in(j, behind_m(j)).wait_recv())
+    near_sum[...] = jnp.sum(near_got[...], axis=0)
+    every(groups, lambda j: far_in(j, h).start())
+    far_got[h] = near_sum[h]
+    every(groups, lambda j: far_in(j, behind_h(j)).wait_recv())
+    totals[m, h] = jnp.sum(far_got[...], axis=0)
+    every(groups, lambda j: far_out(j, h).start())
+    every(groups, lambda j: far_out(j, behind_h(j)).wait_recv())
+    every(4, lambda j: near_out(j, m).start())
+    every(4, lambda j: near_out(j, behind_m(j)).wait_recv())
+    every(4, lambda j: near_in(j, m).wait_send())
+    every(groups, lambda j: far_in(j, h).wait_send())
+    every(groups, lambda j: far_out(j, h).wait_send())
+    every(4, lambda j: near_out(j, m).wait_send())
+
+
+def sum_everywhere(rows):
+    groups = lax.axis_size("seq") * lax.axis_size("dp") // 4
+    size = rows.size
+    tall = -(-size // (groups * 4 * 1024)) * 8
+    padded = jnp.pad(rows.reshape(-1), (0, groups * 4 * tall * 128 - size)).reshape(
+        4, groups, tall, 128
+    )
     vmem = pl.BlockSpec(memory_space=pltpu.VMEM)
     totals = pl.pallas_call(
         sum_kernel,
@@ -347,15 +381,13 @@
         out_specs=vmem,
         scratch_shapes=[
             pltpu.VMEM(padded.shape, jnp.float32),
-            pltpu.SemaphoreType.DMA((2, 2, count)),
+            pltpu.VMEM(padded.shape[1:], jnp.float32),
+            pltpu.VMEM(padded.shape[1:], jnp.float32),
+            pltpu.SemaphoreType.DMA((4, 2, max(groups, 4))),
         ],
         compiler_params=pltpu.CompilerParams(collective_id=1, has_side_effects=True),
-    )(padded).reshape(-1)
-    results, start = [], 0
-    for value in values:
-        results.append(totals[start : start + value.size].reshape(value.shape))
-        start += value.size
-    return results
+    )(padded)
+    return totals.reshape(-1)[:size].reshape(rows.shape)
 
 
 def body(frames, kernel, norm_gain, router, experts, w_in, w_out, cotangent):
@@ -421,7 +453,11 @@
         jnp.bfloat16
     )
     kernel_term = kernel_terms(padded, upstream_total, length, row_count)
-    grad_kernel, grad_gain, grad_router = sum_everywhere((kernel_term, gain_term, router_term))
+    sums = sum_everywhere(
+        jnp.concatenate([kernel_term, gain_term[None], router_term.T], axis=0)
+    )
+    grad_kernel, grad_gain = sums[:length], sums[length]
+    grad_router = sums[length + 1 :].T
     grad_in, grad_out = in_term, out_term
     if lax.axis_size("dp") > 1:
         grad_in, grad_out = (

time: 204 us -> 211 us (1.034)
    pallas_call x1, Pallas kernels: 133 us -> 136 us  [moe(): pl.pallas_call(moe_kernel, out_shape=(jax.ShapeDtypeStruct(packed.shape,...]
    pallas_call x1, Pallas kernels: 24.2 us -> 22 us  [sum_everywhere(): pl.pallas_call(sum_kernel, out_shape=jax.ShapeDtypeStruct(padded.shape, j...]
    unnamed x18 -> x176, local copies, waits for them, and re-layouts: 5.38 us -> 4.86 us
  transfers between devices with their start and end apart: 4 -> 4, of which waited for: 0 -> 1; matrix products, arithmetic and copies ran while one was open for 5% -> 3% of each run, Pallas kernels for 12% -> 0%
where the time goes in v2:
time: 211 us; the launch traced here: 209 us
  Pallas kernels  158 us (75%)
  other arithmetic  21.9 us (10%)
  local copies, waits for them, and re-layouts  13.7 us (6%)
  starting transfers between devices  7.28 us (3%)
  matrix products  4.84 us (2%)
  between operations  2.18 us (1%)
    pallas_call x1, Pallas kernels, moe(): pl.pallas_call(moe_kernel, out_shape=(jax.ShapeDtypeStruct(packed.shape,...  136 us
    pallas_call x1, Pallas kernels, sum_everywhere(): pl.pallas_call(sum_kernel, out_shape=jax.ShapeDtypeStruct(padded.shape, j...  22 us
    reduce_sum x1, other arithmetic, normalize(): square = jnp.mean(summed * summed, axis=-1, keepdims=True)  10.8 us
    unnamed x176, local copies, waits for them, and re-layouts  4.86 us
    ppermute x2, starting transfers between devices, padded_2(): before = lax.ppermute(last, axis, up)  4.7 us
  transfers between devices with their start and end apart: 4, of which 1 were waited for; matrix products, arithmetic and copies ran while one was open for 3% of the time, Pallas kernels for 0%

profile of v2, /device:TPU:0, one launch (start us, length us, event | category | flops | bytes accessed | tf_op | source)
XLA Modules:
  0.0 208.6 jit_solution(17928271085947133272)
XLA Ops:
  0.7 0.8 slice_bitcast_fusion.2
  1.5 2.4 %collective-permute-start = (bf16[15,1024]{1,0:T(8,128)(2,1)S(1)}, bf16[15,1024]{1,0:T(8,128)(2,1)S(1)}, u32[]{:S(2)}, u32[]{:S(2)}) collective-permute-start(bf16[15,1024]{1,0:T(8,128)(2,1)S(1)} %get-tuple-element.63), channel_id=1, source_target_pairs={{0,1},{1,2},{2,3},{3,4},{4,5},{5,6},{6,7},{7,8},{8,9},{9,10},{10,1... | collective-permute-start | bytes 92168 | tf_op jit(solution)/shard_map/ppermute | solution.py:20
  3.9 1.3 collective-permute-start.1
  5.2 1.2 slice_convert_fusion.30
  6.5 1.0 slice_convert_fusion.29
  7.7 0.8 copy.30
  8.5 0.1 eq.77
  8.6 0.1 reshape_squeeze.3
  8.8 0.6 reduce-window.6
  9.4 0.2 slice_reduce_fusion.2
  9.7 0.1 reduce_sum.371
  10.1 0.2 slice_reduce_fusion.1
  10.3 10.8 %multiply_reduce_fusion.2 = (f32[128]{0:T(128)}, f32[128,1024]{1,0:T(8,128)S(1)}) fusion(bf16[15,1024]{1,0:T(8,128)(2,1)S(1)} %collective-permute-done.1, bf16[128,1024]{1,0:T(8,128)(2,1)} %bitcast.142, f32[1024]{0:T(1024)S(1)} %bitcast.216, f32[1024]{0:T(1024)S(1)} %bitcast.218, f32[1024]{0:T(1024)S(1)} %bitcast.160, f32[1024]{0:T(1024)S(1)} %bitcast.162, ...), kind=kLoop, calls=%fused_computation.246 | loop fusion | flops 24248192 | bytes 975360 | tf_op jit(solution)/shard_map/reduce_sum | solution.py:54
  21.1 0.7 fusion.154
  21.9 0.2 fusion
  22.4 0.2 fusion.72
  22.7 0.5 copy.33
  23.2 0.2 convert_element_type.324
  23.4 0.3 broadcast_in_dim.12
  23.7 0.2 reshape.185
  23.9 2.0 convolution_convert_fusion
  26.0 136.4 %shard_map.135 = (bf16[8,64,2048]{2,1,0:T(8,128)(2,1)}, f32[1024,512]{1,0:T(8,128)}, f32[512,1024]{1,0:T(8,128)}) custom-call(bf16[8,64,2048]{2,1,0:T(8,128)(2,1)} %bitcast.141, bf16[1024,512]{1,0:T(8,128)(2,1)} %bitcast.154, bf16[512,1024]{1,0:T(8,128)(2,1)} %bitcast.155), custom_call_target="tpu_custom_call" | custom-call | tf_op jit(solution)/shard_map/pallas_call | solution.py:270
  162.4 1.7 fusion.2
  164.2 0.6 reshape.188
  164.8 0.8 fusion.157
  165.7 1.0 fusion.75
  166.7 0.3 fusion.147
  167.0 0.1 fusion.146
  167.2 0.5 multiply_reduce_fusion
  167.7 0.7 multiply_multiply_fusion
  168.4 0.8 fusion.71
  169.2 0.6 fusion.57
  169.8 0.7 fusion.51
  170.8 0.5 fusion.42
  171.3 0.2 concatenate.48
  171.5 0.7 pad.4
  172.3 22.0 %shard_map.136 = f32[4,8,16,128]{3,2,1,0:T(8,128)} custom-call(f32[4,8,16,128]{3,2,1,0:T(8,128)} %bitcast.153), custom_call_target="tpu_custom_call" | custom-call | tf_op jit(solution)/shard_map/pallas_call | solution.py:377
  194.3 1.0 slice.537
  195.3 2.3 %collective-permute-start.2 = (bf16[15,1024]{1,0:T(8,128)(2,1)S(1)}, bf16[15,1024]{1,0:T(8,128)(2,1)S(1)}, u32[]{:S(2)}, u32[]{:S(2)}) collective-permute-start(bf16[15,1024]{1,0:T(8,128)(2,1)S(1)} %get-tuple-element.59), channel_id=1, source_target_pairs={{0,1},{1,2},{2,3},{3,4},{4,5},{5,6},{6,7},{7,8},{8,9},{9,10},{10,1... | collective-permute-start | bytes 92168 | tf_op jit(solution)/shard_map/ppermute | solution.py:20
  197.7 1.3 collective-permute-start.3
  199.0 0.6 slice_bitcast_fusion
  199.6 0.7 slice.637
  200.2 1.3 slice.638
  201.5 0.3 collective-permute-done.3
  202.2 2.8 %fusion.142 = bf16[1,128,1024]{2,1,0:T(8,128)(2,1)} fusion(f32[128,1024]{1,0:T(8,128)S(1)} %get-tuple-element.50, f32[158,1024]{1,0:T(8,128)S(1)} %maximum_convert_fusion, f32[1024]{0:T(1024)S(1)} %bitcast.217, f32[1024]{0:T(1024)S(1)} %bitcast.219, f32[1024]{0:T(1024)S(1)} %bitcast.161, f32[1024]{0:T(1024)S(1)} %bitcast.163, f32[1024]{0:T(1024)S(1)} %bitcast.165, ...), kind=kLoop, calls=%fused_computation.283 | loop fusion | flops 8257536 | bytes 17166336 | tf_op jit(solution)/shard_map/broadcast_in_dim | solution.py:469
  205.0 1.3 copy.56
  206.3 1.0 copy-done.4
  207.3 1.3 copy.57
  (189 shorter events, 1.0 us)
Async XLA Ops:
  0.6 21.2 %copy-start = (bf16[1024,8]{0,1:T(8,128)(2,1)S(1)}, bf16[1024,8]{0,1:T(8,128)(2,1)}, u32[]{:S(2)}) copy-start(bf16[1024,8]{0,1:T(8,128)(2,1)} %param.11) | copy-start | bytes 49156
  0.6 21.1 %copy-start.10 = (f32[1024]{0:T(1024)S(1)}, f32[1024]{0:T(1024)}, u32[]{:S(2)}) copy-start(f32[1024]{0:T(1024)} %param.10) | copy-start | bytes 12292
  0.7 21.8 %copy-start.2 = (bf16[1,128,1024]{2,1,0:T(8,128)(2,1)S(1)}, bf16[1,128,1024]{2,1,0:T(8,128)(2,1)}, u32[]{:S(2)}) copy-start(bf16[1,128,1024]{2,1,0:T(8,128)(2,1)} %param.15) | copy-start | bytes 786436
  1.5 8.8 %collective-permute-start = (bf16[15,1024]{1,0:T(8,128)(2,1)S(1)}, bf16[15,1024]{1,0:T(8,128)(2,1)S(1)}, u32[]{:S(2)}, u32[]{:S(2)}) collective-permute-start(bf16[15,1024]{1,0:T(8,128)(2,1)S(1)} %get-tuple-element.63), channel_id=1, source_target_pairs={{0,1},{1,2},{2,3},{3,4},{4,5},{5,6},{6,7},{7,8},{8,9},{9,10},{10,1... | collective-permute-start | bytes 92168 | tf_op jit(solution)/shard_map/ppermute | solution.py:20
  3.9 6.4 %collective-permute-start.1 = (bf16[15,1024]{1,0:T(8,128)(2,1)S(1)}, bf16[15,1024]{1,0:T(8,128)(2,1)S(1)}, u32[]{:S(2)}, u32[]{:S(2)}) collective-permute-start(bf16[15,1024]{1,0:T(8,128)(2,1)S(1)} %get-tuple-element.64), channel_id=1, source_target_pairs={{1,0},{2,1},{3,2},{4,3},{5,4},{6,5},{7,6},{8,7},{9,8},{10,9},{11,1... | collective-permute-start | bytes 92168 | tf_op jit(solution)/shard_map/ppermute | solution.py:21
  6.4 15.7 %copy-start.12 = (f32[1,1024]{1,0:T(1,128)}, f32[1,1024]{1,0:T(1,128)S(1)}, u32[]{:S(2)}) copy-start(f32[1,1024]{1,0:T(1,128)S(1)} %get-tuple-element.65) | copy-start | bytes 12292
  6.4 15.7 %copy-start.14 = (f32[1,1024]{1,0:T(1,128)}, f32[1,1024]{1,0:T(1,128)S(1)}, u32[]{:S(2)}) copy-start(f32[1,1024]{1,0:T(1,128)S(1)} %get-tuple-element.66) | copy-start | bytes 12292
  6.4 15.7 %copy-start.16 = (f32[1,1024]{1,0:T(1,128)}, f32[1,1024]{1,0:T(1,128)S(1)}, u32[]{:S(2)}) copy-start(f32[1,1024]{1,0:T(1,128)S(1)} %get-tuple-element.67) | copy-start | bytes 12292
  6.4 15.7 %copy-start.18 = (f32[1,1024]{1,0:T(1,128)}, f32[1,1024]{1,0:T(1,128)S(1)}, u32[]{:S(2)}) copy-start(f32[1,1024]{1,0:T(1,128)S(1)} %get-tuple-element.68) | copy-start | bytes 12292
  6.4 15.7 %copy-start.20 = (f32[1,1024]{1,0:T(1,128)}, f32[1,1024]{1,0:T(1,128)S(1)}, u32[]{:S(2)}) copy-start(f32[1,1024]{1,0:T(1,128)S(1)} %get-tuple-element.69) | copy-start | bytes 12292
  6.4 15.7 %copy-start.22 = (f32[1,1024]{1,0:T(1,128)}, f32[1,1024]{1,0:T(1,128)S(1)}, u32[]{:S(2)}) copy-start(f32[1,1024]{1,0:T(1,128)S(1)} %get-tuple-element.70) | copy-start | bytes 12292
  6.4 15.7 %copy-start.24 = (f32[1,1024]{1,0:T(1,128)}, f32[1,1024]{1,0:T(1,128)S(1)}, u32[]{:S(2)}) copy-start(f32[1,1024]{1,0:T(1,128)S(1)} %get-tuple-element.71) | copy-start | bytes 12292
  6.4 15.7 %copy-start.26 = (f32[1,1024]{1,0:T(1,128)}, f32[1,1024]{1,0:T(1,128)S(1)}, u32[]{:S(2)}) copy-start(f32[1,1024]{1,0:T(1,128)S(1)} %get-tuple-element.72) | copy-start | bytes 12292
  6.4 15.7 %copy-start.28 = (f32[1,1024]{1,0:T(1,128)}, f32[1,1024]{1,0:T(1,128)S(1)}, u32[]{:S(2)}) copy-start(f32[1,1024]{1,0:T(1,128)S(1)} %get-tuple-element.73) | copy-start | bytes 12292
  26.0 136.4 %copy-start.75 = (s32[256]{0:T(256)S(1)}, s32[256]{0:T(256)}, u32[]{:S(2)}) copy-start(s32[256]{0:T(256)} %copy-done.74) | copy-start | bytes 3076
  170.5 31.4 %copy-start.13 = (f32[1,1024]{1,0:T(1,128)S(1)}, f32[1,1024]{1,0:T(1,128)}, u32[]{:S(2)}) copy-start(f32[1,1024]{1,0:T(1,128)} %copy-done.12) | copy-start | bytes 12292
  170.5 31.4 %copy-start.15 = (f32[1,1024]{1,0:T(1,128)S(1)}, f32[1,1024]{1,0:T(1,128)}, u32[]{:S(2)}) copy-start(f32[1,1024]{1,0:T(1,128)} %copy-done.14) | copy-start | bytes 12292
  170.5 31.4 %copy-start.17 = (f32[1,1024]{1,0:T(1,128)S(1)}, f32[1,1024]{1,0:T(1,128)}, u32[]{:S(2)}) copy-start(f32[1,1024]{1,0:T(1,128)} %copy-done.16) | copy-start | bytes 12292
  170.5 31.4 %copy-start.19 = (f32[1,1024]{1,0:T(1,128)S(1)}, f32[1,1024]{1,0:T(1,128)}, u32[]{:S(2)}) copy-start(f32[1,1024]{1,0:T(1,128)} %copy-done.18) | copy-start | bytes 12292
  170.5 31.4 %copy-start.21 = (f32[1,1024]{1,0:T(1,128)S(1)}, f32[1,1024]{1,0:T(1,128)}, u32[]{:S(2)}) copy-start(f32[1,1024]{1,0:T(1,128)} %copy-done.20) | copy-start | bytes 12292
  170.5 31.4 %copy-start.23 = (f32[1,1024]{1,0:T(1,128)S(1)}, f32[1,1024]{1,0:T(1,128)}, u32[]{:S(2)}) copy-start(f32[1,1024]{1,0:T(1,128)} %copy-done.22) | copy-start | bytes 12292
  170.5 31.4 %copy-start.25 = (f32[1,1024]{1,0:T(1,128)S(1)}, f32[1,1024]{1,0:T(1,128)}, u32[]{:S(2)}) copy-start(f32[1,1024]{1,0:T(1,128)} %copy-done.24) | copy-start | bytes 12292
  170.5 31.4 %copy-start.27 = (f32[1,1024]{1,0:T(1,128)S(1)}, f32[1,1024]{1,0:T(1,128)}, u32[]{:S(2)}) copy-start(f32[1,1024]{1,0:T(1,128)} %copy-done.26) | copy-start | bytes 12292
  170.5 31.4 %copy-start.29 = (f32[1,1024]{1,0:T(1,128)S(1)}, f32[1,1024]{1,0:T(1,128)}, u32[]{:S(2)}) copy-start(f32[1,1024]{1,0:T(1,128)} %copy-done.28) | copy-start | bytes 12292
  170.5 31.4 %copy-start.31 = (f32[1,1024]{1,0:T(1,128)S(1)}, f32[1,1024]{1,0:T(1,128)}, u32[]{:S(2)}) copy-start(f32[1,1024]{1,0:T(1,128)} %copy-done.30) | copy-start | bytes 12292
  170.6 31.4 %copy-start.33 = (f32[1,1024]{1,0:T(1,128)S(1)}, f32[1,1024]{1,0:T(1,128)}, u32[]{:S(2)}) copy-start(f32[1,1024]{1,0:T(1,128)} %copy-done.32) | copy-start | bytes 12292
  170.6 31.4 %copy-start.35 = (f32[1,1024]{1,0:T(1,128)S(1)}, f32[1,1024]{1,0:T(1,128)}, u32[]{:S(2)}) copy-start(f32[1,1024]{1,0:T(1,128)} %copy-done.34) | copy-start | bytes 12292
  170.6 31.4 %copy-start.37 = (f32[1,1024]{1,0:T(1,128)S(1)}, f32[1,1024]{1,0:T(1,128)}, u32[]{:S(2)}) copy-start(f32[1,1024]{1,0:T(1,128)} %copy-done.36) | copy-start | bytes 12292
  170.6 31.4 %copy-start.39 = (f32[1,1024]{1,0:T(1,128)S(1)}, f32[1,1024]{1,0:T(1,128)}, u32[]{:S(2)}) copy-start(f32[1,1024]{1,0:T(1,128)} %copy-done.38) | copy-start | bytes 12292
  170.6 31.4 %copy-start.41 = (f32[1,1024]{1,0:T(1,128)S(1)}, f32[1,1024]{1,0:T(1,128)}, u32[]{:S(2)}) copy-start(f32[1,1024]{1,0:T(1,128)} %copy-done.40) | copy-start | bytes 12292
  170.6 31.4 %copy-start.43 = (f32[1,1024]{1,0:T(1,128)S(1)}, f32[1,1024]{1,0:T(1,128)}, u32[]{:S(2)}) copy-start(f32[1,1024]{1,0:T(1,128)} %copy-done.42) | copy-start | bytes 12292
  170.6 31.4 %copy-start.45 = (f32[1,1024]{1,0:T(1,128)S(1)}, f32[1,1024]{1,0:T(1,128)}, u32[]{:S(2)}) copy-start(f32[1,1024]{1,0:T(1,128)} %copy-done.44) | copy-start | bytes 12292
  170.6 31.4 %copy-start.47 = (f32[1,1024]{1,0:T(1,128)S(1)}, f32[1,1024]{1,0:T(1,128)}, u32[]{:S(2)}) copy-start(f32[1,1024]{1,0:T(1,128)} %copy-done.46) | copy-start | bytes 12292
  170.6 31.4 %copy-start.49 = (f32[1,1024]{1,0:T(1,128)S(1)}, f32[1,1024]{1,0:T(1,128)}, u32[]{:S(2)}) copy-start(f32[1,1024]{1,0:T(1,128)} %copy-done.48) | copy-start | bytes 12292
  170.6 31.4 %copy-start.51 = (f32[1,1024]{1,0:T(1,128)S(1)}, f32[1,1024]{1,0:T(1,128)}, u32[]{:S(2)}) copy-start(f32[1,1024]{1,0:T(1,128)} %copy-done.50) | copy-start | bytes 12292
  170.7 31.4 %copy-start.53 = (f32[1,1024]{1,0:T(1,128)S(1)}, f32[1,1024]{1,0:T(1,128)}, u32[]{:S(2)}) copy-start(f32[1,1024]{1,0:T(1,128)} %copy-done.52) | copy-start | bytes 12292
  170.7 31.4 %copy-start.55 = (f32[1,1024]{1,0:T(1,128)S(1)}, f32[1,1024]{1,0:T(1,128)}, u32[]{:S(2)}) copy-start(f32[1,1024]{1,0:T(1,128)} %copy-done.54) | copy-start | bytes 12292
  170.7 31.4 %copy-start.57 = (f32[1,1024]{1,0:T(1,128)S(1)}, f32[1,1024]{1,0:T(1,128)}, u32[]{:S(2)}) copy-start(f32[1,1024]{1,0:T(1,128)} %copy-done.56) | copy-start | bytes 12292
  170.7 31.4 %copy-start.59 = (f32[1,1024]{1,0:T(1,128)S(1)}, f32[1,1024]{1,0:T(1,128)}, u32[]{:S(2)}) copy-start(f32[1,1024]{1,0:T(1,128)} %copy-done.58) | copy-start | bytes 12292
  170.7 31.4 %copy-start.61 = (f32[1,1024]{1,0:T(1,128)S(1)}, f32[1,1024]{1,0:T(1,128)}, u32[]{:S(2)}) copy-start(f32[1,1024]{1,0:T(1,128)} %copy-done.60) | copy-start | bytes 12292
  170.7 31.4 %copy-start.63 = (f32[1,1024]{1,0:T(1,128)S(1)}, f32[1,1024]{1,0:T(1,128)}, u32[]{:S(2)}) copy-start(f32[1,1024]{1,0:T(1,128)} %copy-done.62) | copy-start | bytes 12292
  170.7 31.4 %copy-start.65 = (f32[1,1024]{1,0:T(1,128)S(1)}, f32[1,1024]{1,0:T(1,128)}, u32[]{:S(2)}) copy-start(f32[1,1024]{1,0:T(1,128)} %copy-done.64) | copy-start | bytes 12292
  170.7 31.4 %copy-start.67 = (f32[1,1024]{1,0:T(1,128)S(1)}, f32[1,1024]{1,0:T(1,128)}, u32[]{:S(2)}) copy-start(f32[1,1024]{1,0:T(1,128)} %copy-done.66) | copy-start | bytes 12292
  170.7 31.4 %copy-start.69 = (f32[1,1024]{1,0:T(1,128)S(1)}, f32[1,1024]{1,0:T(1,128)}, u32[]{:S(2)}) copy-start(f32[1,1024]{1,0:T(1,128)} %copy-done.68) | copy-start | bytes 12292
  170.7 31.4 %copy-start.71 = (f32[1,1024]{1,0:T(1,128)S(1)}, f32[1,1024]{1,0:T(1,128)}, u32[]{:S(2)}) copy-start(f32[1,1024]{1,0:T(1,128)} %copy-done.70) | copy-start | bytes 12292
  170.8 31.4 %copy-start.73 = (f32[1,1024]{1,0:T(1,128)S(1)}, f32[1,1024]{1,0:T(1,128)}, u32[]{:S(2)}) copy-start(f32[1,1024]{1,0:T(1,128)} %copy-done.72) | copy-start | bytes 12292
  195.3 6.2 %collective-permute-start.2 = (bf16[15,1024]{1,0:T(8,128)(2,1)S(1)}, bf16[15,1024]{1,0:T(8,128)(2,1)S(1)}, u32[]{:S(2)}, u32[]{:S(2)}) collective-permute-start(bf16[15,1024]{1,0:T(8,128)(2,1)S(1)} %get-tuple-element.59), channel_id=1, source_target_pairs={{0,1},{1,2},{2,3},{3,4},{4,5},{5,6},{6,7},{7,8},{8,9},{9,10},{10,1... | collective-permute-start | bytes 92168 | tf_op jit(solution)/shard_map/ppermute | solution.py:20
  197.7 4.1 %collective-permute-start.3 = (bf16[15,1024]{1,0:T(8,128)(2,1)S(1)}, bf16[15,1024]{1,0:T(8,128)(2,1)S(1)}, u32[]{:S(2)}, u32[]{:S(2)}) collective-permute-start(bf16[15,1024]{1,0:T(8,128)(2,1)S(1)} %get-tuple-element.60), channel_id=1, source_target_pairs={{1,0},{2,1},{3,2},{4,3},{5,4},{6,5},{7,6},{8,7},{9,8},{10,9},{11,1... | collective-permute-start | bytes 92168 | tf_op jit(solution)/shard_map/ppermute | solution.py:21
  (42 other events, 423.7 us)

commit v3 on v2

--- a/solution.py
+++ b/solution.py
@@ -23,13 +23,56 @@
     return shard
 
 
-def conv_forward(padded, kernel, row_count):
-    summed = jnp.zeros((row_count, padded.shape[1]), jnp.float32)
-    for offset in range(kernel.shape[0]):
-        summed = summed + kernel[offset].astype(jnp.float32) * padded[
-            offset : offset + row_count
-        ].astype(jnp.float32)
-    return summed
+def conv_norm_kernel(padded, kernel, gain, summed, normed, wide):
+    row_count, width = summed.shape
+    length = kernel.shape[0]
+    wide[: padded.shape[0]] = padded[...].astype(jnp.float32)
+
+    def columns(i):
+        return pl.ds(pl.multiple_of(i * 128, 128), 128)
+
+    def convolve(i, square):
+        at = columns(i)
+        total = jnp.zeros((row_count, 128), jnp.float32)
+        for offset in range(length):
+            weight = kernel[offset : offset + 1, at].astype(jnp.float32)
+            total = total + weight * wide[offset : offset + row_count, at]
+        total = wide[length // 2 : length // 2 + row_count, at] + total
+        summed[:, at] = total
+        return square + total * total
+
+    square = lax.fori_loop(
+        0, width // 128, convolve, jnp.zeros((row_count, 128), jnp.float32)
+    )
+    scale = lax.rsqrt(jnp.sum(square, axis=1, keepdims=True) / width + eps)
+
+    def apply(i, carry):
+        at = columns(i)
+        normed[:, at] = (summed[:, at] * scale * gain[:, at]).astype(jnp.bfloat16)
+        return carry
+
+    lax.fori_loop(0, width // 128, apply, 0)
+
+
+def conv_norm(padded, kernel, norm_gain, row_count):
+    width = padded.shape[1]
+    tall = -(-padded.shape[0] // 16) * 16
+    vmem = pl.BlockSpec(memory_space=pltpu.VMEM)
+    return pl.pallas_call(
+        conv_norm_kernel,
+        out_shape=(
+            jax.ShapeDtypeStruct((row_count, width), jnp.float32),
+            jax.ShapeDtypeStruct((row_count, width), jnp.bfloat16),
+        ),
+        in_specs=[vmem] * 3,
+        out_specs=(vmem,) * 2,
+        scratch_shapes=[pltpu.VMEM((tall, width), jnp.float32)],
+        compiler_params=pltpu.CompilerParams(vmem_limit_bytes=12 * 2**20),
+    )(
+        jnp.pad(padded, ((0, tall - padded.shape[0]), (0, 0))),
+        kernel.astype(jnp.float32),
+        norm_gain[None],
+    )
 
 
 def conv_transpose(padded, kernel, row_count):
@@ -164,7 +207,8 @@
         dispatch(k).start()
         return carry
 
-    lax.fori_loop(1, count, send_first, 0)
+    ahead = min(4, count)
+    lax.fori_loop(1, ahead, send_first, 0)
     rows[e, own] = packed[e]
     grad_in[...] = jnp.zeros_like(grad_in)
     grad_out[...] = jnp.zeros_like(grad_out)
@@ -178,6 +222,10 @@
 
         near(1, k, own, x_peer).start()
         near(2, k, own, core_peer).start()
+
+        @pl.when(k + ahead < count)
+        def _():
+            dispatch(k + ahead).start()
 
     def stage_forward(k):
         near(1, k, own_x, x_peer).wait_recv()
@@ -229,9 +277,9 @@
     stages = (
         (4, stage_back),
         (3, stage_core),
+        (2, stage_compute),
         (1, stage_forward),
         (0, stage_spread),
-        (2, stage_compute),
     )
 
     def step(t, carry):
@@ -402,8 +450,7 @@
     in_weights = w_in[0]
     out_weights = w_out[0]
     padded = padded_2(inputs_dev, (("seq", 0),), half_width)
-    summed = inputs_dev.astype(jnp.float32) + conv_forward(padded, kernel, row_count)
-    normed_b = normalize(summed, norm_gain).astype(jnp.bfloat16)
+    summed, normed_b = conv_norm(padded, kernel, norm_gain, row_count)
     choice_ids = experts[0]
     gate_one, gate_two, pick_diff = gate_values(
         normed_b, router, choice_ids[:, 0], choice_ids[:, 1]

time: 211 us -> 200 us (0.948)
  other arithmetic: 21.9 us -> 13.5 us
    reduce_sum x1 -> x0, other arithmetic: 10.8 us -> none  [normalize(): square = jnp.mean(summed * summed, axis=-1, keepdims=True)]
    pallas_call x1, Pallas kernels: 136 us -> 133 us  [moe(): pl.pallas_call(moe_kernel, out_shape=(jax.ShapeDtypeStruct(packed.shape,...]
    pallas_call x0 -> x1, Pallas kernels: none -> 2.92 us  [conv_norm(): pl.pallas_call(conv_norm_kernel, out_shape=(jax.ShapeDtypeStruct((row_cou...]
    unnamed x176 -> x70, local copies, waits for them, and re-layouts: 4.86 us -> 4.9 us
  transfers between devices with their start and end apart: 4 -> 4, of which waited for: 1 -> 0; matrix products, arithmetic and copies ran while one was open for 3% -> 5% of each run, Pallas kernels for 0% -> 0%
where the time goes in v3:
time: 200 us; the launch traced here: 197 us
  Pallas kernels  156 us (78%)
  local copies, waits for them, and re-layouts  13.8 us (7%)
  other arithmetic  13.5 us (7%)
  starting transfers between devices  7.36 us (4%)
  matrix products  4.84 us (2%)
    pallas_call x1, Pallas kernels, moe(): pl.pallas_call(moe_kernel, out_shape=(jax.ShapeDtypeStruct(packed.shape,...  133 us
    pallas_call x1, Pallas kernels, sum_everywhere(): pl.pallas_call(sum_kernel, out_shape=jax.ShapeDtypeStruct(padded.shape, j...  20.6 us
    unnamed x70, local copies, waits for them, and re-layouts  4.9 us
    ppermute x2, starting transfers between devices, padded_2(): before = lax.ppermute(last, axis, up)  4.78 us
  transfers between devices with their start and end apart: 4, of which 0 were waited for; matrix products, arithmetic and copies ran while one was open for 5% of the time, Pallas kernels for 0%

profile of v3, /device:TPU:0, one launch (start us, length us, event | category | flops | bytes accessed | tf_op | source)
XLA Modules:
  0.0 197.2 jit_solution(12517405867760019043)
XLA Ops:
  0.7 0.8 slice_bitcast_fusion.2
  1.5 2.4 %collective-permute-start = (bf16[15,1024]{1,0:T(8,128)(2,1)S(1)}, bf16[15,1024]{1,0:T(8,128)(2,1)S(1)}, u32[]{:S(2)}, u32[]{:S(2)}) collective-permute-start(bf16[15,1024]{1,0:T(8,128)(2,1)S(1)} %get-tuple-element.66), channel_id=1, source_target_pairs={{0,1},{1,2},{2,3},{3,4},{4,5},{5,6},{6,7},{7,8},{8,9},{9,10},{10,1... | collective-permute-start | bytes 92168 | tf_op jit(solution)/shard_map/ppermute | solution.py:20
  3.9 1.3 collective-permute-start.1
  5.2 0.8 copy.28
  6.0 0.1 eq.77
  6.1 0.1 reshape_squeeze.3
  6.3 0.6 reduce-window.6
  6.8 0.2 slice_reduce_fusion.2
  7.3 1.8 slice_convert_fusion.30
  9.2 1.6 slice_convert_fusion.29
  10.8 0.7 fusion.54
  11.6 0.2 slice_reduce_fusion.1
  11.8 0.9 convert_element_type.225.kernel
  12.7 1.0 fusion.53.padded
  13.7 2.9 %shard_map.135 = (f32[128,1024]{1,0:T(8,128)S(1)}, bf16[128,1024]{1,0:T(8,128)(2,1)S(1)}) custom-call(bf16[160,1024]{1,0:T(8,128)(2,1)S(1)} %fusion.53.padded, f32[31,1024]{1,0:T(8,128)S(1)} %convert_element_type.225.kernel, f32[1,1024]{1,0:T(1,128)S(1)} %bitcast.142), custom_call_target="tpu_custom_call" | custom-call | tf_op jit(solution)/shard_map/pallas_call | solution.py:61
  16.7 0.2 fusion
  16.9 0.2 fusion.15
  17.1 0.3 copy-done.29
  17.4 0.5 copy.31
  17.9 0.2 convert_element_type.232
  18.1 0.3 broadcast_in_dim.15
  18.4 0.2 reshape.185
  18.6 2.0 %convolution_convert_fusion = bf16[512,2048]{1,0:T(8,128)(2,1)} fusion(bf16[256,1024]{1,0:T(8,128)(2,1)S(1)} %convert_element_type.232, bf16[256,1024]{1,0:T(8,128)(2,1)S(1)} %reshape.185, s32[256]{0:T(256)S(1)} %multiply_add_fusion.1), kind=kOutput, calls=%fused_computation | convolution fusion | flops 540147712 | bytes 3146752 | tf_op jit(solution)/shard_map/dot_general | solution.py:467
  20.7 132.9 %shard_map.136 = (bf16[8,64,2048]{2,1,0:T(8,128)(2,1)}, f32[1024,512]{1,0:T(8,128)}, f32[512,1024]{1,0:T(8,128)}) custom-call(bf16[8,64,2048]{2,1,0:T(8,128)(2,1)} %bitcast.143, bf16[1024,512]{1,0:T(8,128)(2,1)} %bitcast.156, bf16[512,1024]{1,0:T(8,128)(2,1)} %bitcast.157), custom_call_target="tpu_custom_call" | custom-call | tf_op jit(solution)/shard_map/pallas_call | solution.py:318
  153.6 1.7 fusion.2
  155.3 0.6 reshape.188
  156.0 0.8 fusion.101
  156.8 1.1 fusion.18
  157.9 0.3 fusion.91
  158.2 0.1 fusion.90
  158.4 0.5 multiply_reduce_fusion
  158.9 0.8 multiply_reduce_fusion.1
  159.7 0.6 multiply_reduce_fusion.10
  160.3 0.7 multiply_reduce_fusion.17
  161.0 0.5 multiply_reduce_fusion.26
  161.6 0.2 concatenate.51
  161.9 0.7 pad.9
  162.6 20.6 %shard_map.137 = f32[4,8,16,128]{3,2,1,0:T(8,128)} custom-call(f32[4,8,16,128]{3,2,1,0:T(8,128)} %bitcast.155), custom_call_target="tpu_custom_call" | custom-call | tf_op jit(solution)/shard_map/pallas_call | solution.py:425
  183.2 1.0 slice.476
  184.2 2.4 %collective-permute-start.2 = (bf16[15,1024]{1,0:T(8,128)(2,1)S(1)}, bf16[15,1024]{1,0:T(8,128)(2,1)S(1)}, u32[]{:S(2)}, u32[]{:S(2)}) collective-permute-start(bf16[15,1024]{1,0:T(8,128)(2,1)S(1)} %get-tuple-element.62), channel_id=1, source_target_pairs={{0,1},{1,2},{2,3},{3,4},{4,5},{5,6},{6,7},{7,8},{8,9},{9,10},{10,1... | collective-permute-start | bytes 92168 | tf_op jit(solution)/shard_map/ppermute | solution.py:20
  186.7 1.3 collective-permute-start.3
  188.0 0.6 slice_bitcast_fusion
  188.6 0.7 slice.576
  189.2 1.3 slice.577
  190.8 2.8 %fusion.86 = bf16[1,128,1024]{2,1,0:T(8,128)(2,1)} fusion(f32[128,1024]{1,0:T(8,128)S(1)} %get-tuple-element.54, f32[158,1024]{1,0:T(8,128)S(1)} %maximum_convert_fusion, f32[1024]{0:T(1024)S(1)} %bitcast.221, f32[1024]{0:T(1024)S(1)} %bitcast.222, f32[1024]{0:T(1024)S(1)} %bitcast.193, f32[1024]{0:T(1024)S(1)} %bitcast.194, f32[1024]{0:T(1024)S(1)} %bitcast.195, ...), kind=kLoop, calls=%fused_computation.195 | loop fusion | flops 8257536 | bytes 17166336 | tf_op jit(solution)/shard_map/broadcast_in_dim | solution.py:516
  193.6 1.3 copy.54
  194.9 1.0 copy-done.5
  195.9 1.3 copy.55
  (83 shorter events, 0.7 us)
Async XLA Ops:
  0.6 16.0 %copy-start = (bf16[1024,8]{0,1:T(8,128)(2,1)S(1)}, bf16[1024,8]{0,1:T(8,128)(2,1)}, u32[]{:S(2)}) copy-start(bf16[1024,8]{0,1:T(8,128)(2,1)} %param.11) | copy-start | bytes 49156
  0.6 13.1 %copy-start.1 = (f32[1024]{0:T(1024)S(1)}, f32[1024]{0:T(1024)}, u32[]{:S(2)}) copy-start(f32[1024]{0:T(1024)} %param.10) | copy-start | bytes 12292
  0.7 16.3 %copy-start.3 = (bf16[1,128,1024]{2,1,0:T(8,128)(2,1)S(1)}, bf16[1,128,1024]{2,1,0:T(8,128)(2,1)}, u32[]{:S(2)}) copy-start(bf16[1,128,1024]{2,1,0:T(8,128)(2,1)} %param.15) | copy-start | bytes 786436
  1.5 11.1 %collective-permute-start = (bf16[15,1024]{1,0:T(8,128)(2,1)S(1)}, bf16[15,1024]{1,0:T(8,128)(2,1)S(1)}, u32[]{:S(2)}, u32[]{:S(2)}) collective-permute-start(bf16[15,1024]{1,0:T(8,128)(2,1)S(1)} %get-tuple-element.66), channel_id=1, source_target_pairs={{0,1},{1,2},{2,3},{3,4},{4,5},{5,6},{6,7},{7,8},{8,9},{9,10},{10,1... | collective-permute-start | bytes 92168 | tf_op jit(solution)/shard_map/ppermute | solution.py:20
  3.9 8.8 %collective-permute-start.1 = (bf16[15,1024]{1,0:T(8,128)(2,1)S(1)}, bf16[15,1024]{1,0:T(8,128)(2,1)S(1)}, u32[]{:S(2)}, u32[]{:S(2)}) collective-permute-start(bf16[15,1024]{1,0:T(8,128)(2,1)S(1)} %get-tuple-element.67), channel_id=1, source_target_pairs={{1,0},{2,1},{3,2},{4,3},{5,4},{6,5},{7,6},{8,7},{9,8},{10,9},{11,1... | collective-permute-start | bytes 92168 | tf_op jit(solution)/shard_map/ppermute | solution.py:21
  11.8 5.1 %copy-start.25 = (s32[128]{0:T(128)}, s32[128]{0:T(128)S(1)}, u32[]{:S(2)}) copy-start(s32[128]{0:T(128)S(1)} %get-tuple-element.52) | copy-start | bytes 1540
  11.8 5.1 %copy-start.27 = (s32[128]{0:T(128)}, s32[128]{0:T(128)S(1)}, u32[]{:S(2)}) copy-start(s32[128]{0:T(128)S(1)} %get-tuple-element.53) | copy-start | bytes 1540
  16.9 0.5 copy-start.29
  16.9 0.5 copy-start.31
  155.3 1.5 copy-start.30
  155.3 1.5 copy-start.32
  156.0 2.0 copy-start.26
  156.0 2.0 copy-start.28
  156.0 2.4 %copy-start.4 = (bf16[8,64,2048]{2,1,0:T(8,128)(2,1)S(1)}, bf16[8,64,2048]{2,1,0:T(8,128)(2,1)}, u32[]{:S(2)}) copy-start(bf16[8,64,2048]{2,1,0:T(8,128)(2,1)} %get-tuple-element.14) | copy-start | bytes 6291460
  156.0 2.4 %copy-start.7 = (bf16[512,128]{1,0:T(8,128)(2,1)S(1)}, bf16[512,128]{1,0:T(8,128)(2,1)}, u32[]{:S(2)}) copy-start(bf16[512,128]{1,0:T(8,128)(2,1)} %fusion.54) | copy-start | bytes 393220
  157.9 1.0 copy-start.2
  161.4 29.2 %copy-start.8 = (f32[1,1024]{1,0:T(1,128)S(1)}, f32[1,1024]{1,0:T(1,128)}, u32[]{:S(2)}) copy-start(f32[1,1024]{1,0:T(1,128)} %get-tuple-element.82) | copy-start | bytes 12292
  161.5 29.2 %copy-start.9 = (f32[1,1024]{1,0:T(1,128)S(1)}, f32[1,1024]{1,0:T(1,128)}, u32[]{:S(2)}) copy-start(f32[1,1024]{1,0:T(1,128)} %get-tuple-element.83) | copy-start | bytes 12292
  161.5 29.2 %copy-start.10 = (f32[1,1024]{1,0:T(1,128)S(1)}, f32[1,1024]{1,0:T(1,128)}, u32[]{:S(2)}) copy-start(f32[1,1024]{1,0:T(1,128)} %get-tuple-element.84) | copy-start | bytes 12292
  161.5 29.2 %copy-start.11 = (f32[1,1024]{1,0:T(1,128)S(1)}, f32[1,1024]{1,0:T(1,128)}, u32[]{:S(2)}) copy-start(f32[1,1024]{1,0:T(1,128)} %get-tuple-element.85) | copy-start | bytes 12292
  161.5 29.2 %copy-start.12 = (f32[1,1024]{1,0:T(1,128)S(1)}, f32[1,1024]{1,0:T(1,128)}, u32[]{:S(2)}) copy-start(f32[1,1024]{1,0:T(1,128)} %get-tuple-element.86) | copy-start | bytes 12292
  161.5 29.2 %copy-start.13 = (f32[1,1024]{1,0:T(1,128)S(1)}, f32[1,1024]{1,0:T(1,128)}, u32[]{:S(2)}) copy-start(f32[1,1024]{1,0:T(1,128)} %get-tuple-element.87) | copy-start | bytes 12292
  161.5 29.2 %copy-start.14 = (f32[1,1024]{1,0:T(1,128)S(1)}, f32[1,1024]{1,0:T(1,128)}, u32[]{:S(2)}) copy-start(f32[1,1024]{1,0:T(1,128)} %get-tuple-element.88) | copy-start | bytes 12292
  161.5 29.2 %copy-start.15 = (f32[1,1024]{1,0:T(1,128)S(1)}, f32[1,1024]{1,0:T(1,128)}, u32[]{:S(2)}) copy-start(f32[1,1024]{1,0:T(1,128)} %get-tuple-element.89) | copy-start | bytes 12292
  161.5 29.2 %copy-start.16 = (f32[1,1024]{1,0:T(1,128)S(1)}, f32[1,1024]{1,0:T(1,128)}, u32[]{:S(2)}) copy-start(f32[1,1024]{1,0:T(1,128)} %get-tuple-element.90) | copy-start | bytes 12292
  161.5 29.2 %copy-start.17 = (f32[1,1024]{1,0:T(1,128)S(1)}, f32[1,1024]{1,0:T(1,128)}, u32[]{:S(2)}) copy-start(f32[1,1024]{1,0:T(1,128)} %get-tuple-element.91) | copy-start | bytes 12292
  161.5 29.2 %copy-start.18 = (f32[1,1024]{1,0:T(1,128)S(1)}, f32[1,1024]{1,0:T(1,128)}, u32[]{:S(2)}) copy-start(f32[1,1024]{1,0:T(1,128)} %get-tuple-element.92) | copy-start | bytes 12292
  161.6 29.2 %copy-start.19 = (f32[1,1024]{1,0:T(1,128)S(1)}, f32[1,1024]{1,0:T(1,128)}, u32[]{:S(2)}) copy-start(f32[1,1024]{1,0:T(1,128)} %get-tuple-element.93) | copy-start | bytes 12292
  161.6 29.2 %copy-start.20 = (f32[1,1024]{1,0:T(1,128)S(1)}, f32[1,1024]{1,0:T(1,128)}, u32[]{:S(2)}) copy-start(f32[1,1024]{1,0:T(1,128)} %get-tuple-element.94) | copy-start | bytes 12292
  161.6 29.2 %copy-start.21 = (f32[1,1024]{1,0:T(1,128)S(1)}, f32[1,1024]{1,0:T(1,128)}, u32[]{:S(2)}) copy-start(f32[1,1024]{1,0:T(1,128)} %get-tuple-element.95) | copy-start | bytes 12292
  161.6 29.2 %copy-start.22 = (f32[1,1024]{1,0:T(1,128)S(1)}, f32[1,1024]{1,0:T(1,128)}, u32[]{:S(2)}) copy-start(f32[1,1024]{1,0:T(1,128)} %get-tuple-element.96) | copy-start | bytes 12292
  161.6 29.2 %copy-start.23 = (f32[1,1024]{1,0:T(1,128)S(1)}, f32[1,1024]{1,0:T(1,128)}, u32[]{:S(2)}) copy-start(f32[1,1024]{1,0:T(1,128)} %get-tuple-element.97) | copy-start | bytes 12292
  161.6 29.2 %copy-start.24 = (f32[1,1024]{1,0:T(1,128)S(1)}, f32[1,1024]{1,0:T(1,128)}, u32[]{:S(2)}) copy-start(f32[1,1024]{1,0:T(1,128)} %get-tuple-element.98) | copy-start | bytes 12292
  184.2 6.3 %collective-permute-start.2 = (bf16[15,1024]{1,0:T(8,128)(2,1)S(1)}, bf16[15,1024]{1,0:T(8,128)(2,1)S(1)}, u32[]{:S(2)}, u32[]{:S(2)}) collective-permute-start(bf16[15,1024]{1,0:T(8,128)(2,1)S(1)} %get-tuple-element.62), channel_id=1, source_target_pairs={{0,1},{1,2},{2,3},{3,4},{4,5},{5,6},{6,7},{7,8},{8,9},{9,10},{10,1... | collective-permute-start | bytes 92168 | tf_op jit(solution)/shard_map/ppermute | solution.py:20
  186.7 3.9 %collective-permute-start.3 = (bf16[15,1024]{1,0:T(8,128)(2,1)S(1)}, bf16[15,1024]{1,0:T(8,128)(2,1)S(1)}, u32[]{:S(2)}, u32[]{:S(2)}) collective-permute-start(bf16[15,1024]{1,0:T(8,128)(2,1)S(1)} %get-tuple-element.63), channel_id=1, source_target_pairs={{1,0},{2,1},{3,2},{4,3},{5,4},{6,5},{7,6},{8,7},{9,8},{10,9},{11,1... | collective-permute-start | bytes 92168 | tf_op jit(solution)/shard_map/ppermute | solution.py:21
  190.8 2.8 %copy-start.6 = (f32[1024,512]{1,0:T(8,128)S(1)}, f32[1024,512]{1,0:T(8,128)}, u32[]{:S(2)}) copy-start(f32[1024,512]{1,0:T(8,128)} %get-tuple-element.15) | copy-start | bytes 6291460
  193.6 2.3 %copy-start.5 = (f32[512,1024]{1,0:T(8,128)S(1)}, f32[512,1024]{1,0:T(8,128)}, u32[]{:S(2)}) copy-start(f32[512,1024]{1,0:T(8,128)} %get-tuple-element.16) | copy-start | bytes 6291460

commit v4 on v3

--- a/solution.py
+++ b/solution.py
@@ -275,10 +275,10 @@
             give_back(k, e).start()
 
     stages = (
-        (4, stage_back),
-        (3, stage_core),
-        (2, stage_compute),
         (1, stage_forward),
+        (3, stage_back),
+        (2, stage_core),
+        (1, stage_compute),
         (0, stage_spread),
     )
 
@@ -292,7 +292,7 @@
 
         return carry
 
-    lax.fori_loop(0, count + 4, step, 0)
+    lax.fori_loop(0, count + 3, step, 0)
 
     def finish(k, carry):
         @pl.when(k > 0)

time: 200 us -> 202 us (1.010)
  Pallas kernels: 156 us -> 159 us
where the time goes in v4:
time: 202 us; the launch traced here: 199 us
  Pallas kernels  159 us (79%)
  local copies, waits for them, and re-layouts  13.8 us (7%)
  other arithmetic  13.5 us (7%)
  starting transfers between devices  7.36 us (4%)
  matrix products  4.84 us (2%)
    pallas_call x1, Pallas kernels, moe(): pl.pallas_call(moe_kernel, out_shape=(jax.ShapeDtypeStruct(packed.shape,...  134 us
    pallas_call x1, Pallas kernels, sum_everywhere(): pl.pallas_call(sum_kernel, out_shape=jax.ShapeDtypeStruct(padded.shape, j...  21.2 us
    unnamed x70, local copies, waits for them, and re-layouts  4.9 us
    ppermute x2, starting transfers between devices, padded_2(): before = lax.ppermute(last, axis, up)  4.78 us
  transfers between devices with their start and end apart: 4, of which 0 were waited for; matrix products, arithmetic and copies ran while one was open for 5% of the time, Pallas kernels for 0%

profile of v4, /device:TPU:0, one launch (start us, length us, event | category | flops | bytes accessed | tf_op | source)
XLA Modules:
  0.0 199.4 jit_solution(14031975756816211331)
XLA Ops:
  0.7 0.8 slice_bitcast_fusion.2
  1.5 2.4 %collective-permute-start = (bf16[15,1024]{1,0:T(8,128)(2,1)S(1)}, bf16[15,1024]{1,0:T(8,128)(2,1)S(1)}, u32[]{:S(2)}, u32[]{:S(2)}) collective-permute-start(bf16[15,1024]{1,0:T(8,128)(2,1)S(1)} %get-tuple-element.66), channel_id=1, source_target_pairs={{0,1},{1,2},{2,3},{3,4},{4,5},{5,6},{6,7},{7,8},{8,9},{9,10},{10,1... | collective-permute-start | bytes 92168 | tf_op jit(solution)/shard_map/ppermute | solution.py:20
  3.9 1.3 collective-permute-start.1
  5.2 0.8 copy.28
  6.0 0.1 eq.77
  6.1 0.1 reshape_squeeze.3
  6.3 0.6 reduce-window.6
  6.8 0.2 slice_reduce_fusion.2
  7.3 1.8 slice_convert_fusion.30
  9.2 1.6 slice_convert_fusion.29
  10.8 0.7 fusion.54
  11.6 0.2 slice_reduce_fusion.1
  11.8 0.9 convert_element_type.225.kernel
  12.7 1.0 fusion.53.padded
  13.7 2.9 %shard_map.135 = (f32[128,1024]{1,0:T(8,128)S(1)}, bf16[128,1024]{1,0:T(8,128)(2,1)S(1)}) custom-call(bf16[160,1024]{1,0:T(8,128)(2,1)S(1)} %fusion.53.padded, f32[31,1024]{1,0:T(8,128)S(1)} %convert_element_type.225.kernel, f32[1,1024]{1,0:T(1,128)S(1)} %bitcast.142), custom_call_target="tpu_custom_call" | custom-call | tf_op jit(solution)/shard_map/pallas_call | solution.py:61
  16.7 0.2 fusion
  16.9 0.2 fusion.15
  17.1 0.3 copy-done.29
  17.4 0.5 copy.31
  17.9 0.2 convert_element_type.232
  18.1 0.3 broadcast_in_dim.15
  18.4 0.2 reshape.185
  18.6 2.0 %convolution_convert_fusion = bf16[512,2048]{1,0:T(8,128)(2,1)} fusion(bf16[256,1024]{1,0:T(8,128)(2,1)S(1)} %convert_element_type.232, bf16[256,1024]{1,0:T(8,128)(2,1)S(1)} %reshape.185, s32[256]{0:T(256)S(1)} %multiply_add_fusion.1), kind=kOutput, calls=%fused_computation | convolution fusion | flops 540147712 | bytes 3146752 | tf_op jit(solution)/shard_map/dot_general | solution.py:467
  20.7 134.5 %shard_map.136 = (bf16[8,64,2048]{2,1,0:T(8,128)(2,1)}, f32[1024,512]{1,0:T(8,128)}, f32[512,1024]{1,0:T(8,128)}) custom-call(bf16[8,64,2048]{2,1,0:T(8,128)(2,1)} %bitcast.143, bf16[1024,512]{1,0:T(8,128)(2,1)} %bitcast.156, bf16[512,1024]{1,0:T(8,128)(2,1)} %bitcast.157), custom_call_target="tpu_custom_call" | custom-call | tf_op jit(solution)/shard_map/pallas_call | solution.py:318
  155.1 1.7 fusion.2
  156.9 0.6 reshape.188
  157.6 0.8 fusion.101
  158.4 1.1 fusion.18
  159.5 0.3 fusion.91
  159.8 0.1 fusion.90
  159.9 0.5 multiply_reduce_fusion
  160.4 0.8 multiply_reduce_fusion.1
  161.3 0.6 multiply_reduce_fusion.10
  161.8 0.7 multiply_reduce_fusion.17
  162.5 0.5 multiply_reduce_fusion.26
  163.2 0.2 concatenate.51
  163.5 0.7 pad.9
  164.2 21.2 %shard_map.137 = f32[4,8,16,128]{3,2,1,0:T(8,128)} custom-call(f32[4,8,16,128]{3,2,1,0:T(8,128)} %bitcast.155), custom_call_target="tpu_custom_call" | custom-call | tf_op jit(solution)/shard_map/pallas_call | solution.py:425
  185.4 1.0 slice.476
  186.4 2.4 %collective-permute-start.2 = (bf16[15,1024]{1,0:T(8,128)(2,1)S(1)}, bf16[15,1024]{1,0:T(8,128)(2,1)S(1)}, u32[]{:S(2)}, u32[]{:S(2)}) collective-permute-start(bf16[15,1024]{1,0:T(8,128)(2,1)S(1)} %get-tuple-element.62), channel_id=1, source_target_pairs={{0,1},{1,2},{2,3},{3,4},{4,5},{5,6},{6,7},{7,8},{8,9},{9,10},{10,1... | collective-permute-start | bytes 92168 | tf_op jit(solution)/shard_map/ppermute | solution.py:20
  188.8 1.3 collective-permute-start.3
  190.1 0.6 slice_bitcast_fusion
  190.8 0.7 slice.576
  191.4 1.3 slice.577
  193.0 2.8 %fusion.86 = bf16[1,128,1024]{2,1,0:T(8,128)(2,1)} fusion(f32[128,1024]{1,0:T(8,128)S(1)} %get-tuple-element.54, f32[158,1024]{1,0:T(8,128)S(1)} %maximum_convert_fusion, f32[1024]{0:T(1024)S(1)} %bitcast.221, f32[1024]{0:T(1024)S(1)} %bitcast.222, f32[1024]{0:T(1024)S(1)} %bitcast.193, f32[1024]{0:T(1024)S(1)} %bitcast.194, f32[1024]{0:T(1024)S(1)} %bitcast.195, ...), kind=kLoop, calls=%fused_computation.195 | loop fusion | flops 8257536 | bytes 17166336 | tf_op jit(solution)/shard_map/broadcast_in_dim | solution.py:516
  195.7 1.3 copy.54
  197.1 1.0 copy-done.5
  198.1 1.3 copy.55
  (83 shorter events, 0.7 us)
Async XLA Ops:
  0.6 16.0 %copy-start = (bf16[1024,8]{0,1:T(8,128)(2,1)S(1)}, bf16[1024,8]{0,1:T(8,128)(2,1)}, u32[]{:S(2)}) copy-start(bf16[1024,8]{0,1:T(8,128)(2,1)} %param.11) | copy-start | bytes 49156
  0.6 13.1 %copy-start.1 = (f32[1024]{0:T(1024)S(1)}, f32[1024]{0:T(1024)}, u32[]{:S(2)}) copy-start(f32[1024]{0:T(1024)} %param.10) | copy-start | bytes 12292
  0.7 16.3 %copy-start.3 = (bf16[1,128,1024]{2,1,0:T(8,128)(2,1)S(1)}, bf16[1,128,1024]{2,1,0:T(8,128)(2,1)}, u32[]{:S(2)}) copy-start(bf16[1,128,1024]{2,1,0:T(8,128)(2,1)} %param.15) | copy-start | bytes 786436
  1.5 11.1 %collective-permute-start = (bf16[15,1024]{1,0:T(8,128)(2,1)S(1)}, bf16[15,1024]{1,0:T(8,128)(2,1)S(1)}, u32[]{:S(2)}, u32[]{:S(2)}) collective-permute-start(bf16[15,1024]{1,0:T(8,128)(2,1)S(1)} %get-tuple-element.66), channel_id=1, source_target_pairs={{0,1},{1,2},{2,3},{3,4},{4,5},{5,6},{6,7},{7,8},{8,9},{9,10},{10,1... | collective-permute-start | bytes 92168 | tf_op jit(solution)/shard_map/ppermute | solution.py:20
  3.9 8.8 %collective-permute-start.1 = (bf16[15,1024]{1,0:T(8,128)(2,1)S(1)}, bf16[15,1024]{1,0:T(8,128)(2,1)S(1)}, u32[]{:S(2)}, u32[]{:S(2)}) collective-permute-start(bf16[15,1024]{1,0:T(8,128)(2,1)S(1)} %get-tuple-element.67), channel_id=1, source_target_pairs={{1,0},{2,1},{3,2},{4,3},{5,4},{6,5},{7,6},{8,7},{9,8},{10,9},{11,1... | collective-permute-start | bytes 92168 | tf_op jit(solution)/shard_map/ppermute | solution.py:21
  11.8 5.1 %copy-start.25 = (s32[128]{0:T(128)}, s32[128]{0:T(128)S(1)}, u32[]{:S(2)}) copy-start(s32[128]{0:T(128)S(1)} %get-tuple-element.52) | copy-start | bytes 1540
  11.8 5.1 %copy-start.27 = (s32[128]{0:T(128)}, s32[128]{0:T(128)S(1)}, u32[]{:S(2)}) copy-start(s32[128]{0:T(128)S(1)} %get-tuple-element.53) | copy-start | bytes 1540
  16.9 0.5 copy-start.29
  16.9 0.5 copy-start.31
  156.9 1.5 copy-start.30
  156.9 1.5 copy-start.32
  157.5 2.0 copy-start.26
  157.5 2.0 copy-start.28
  157.5 2.4 %copy-start.4 = (bf16[8,64,2048]{2,1,0:T(8,128)(2,1)S(1)}, bf16[8,64,2048]{2,1,0:T(8,128)(2,1)}, u32[]{:S(2)}) copy-start(bf16[8,64,2048]{2,1,0:T(8,128)(2,1)} %get-tuple-element.14) | copy-start | bytes 6291460
  157.5 2.4 %copy-start.7 = (bf16[512,128]{1,0:T(8,128)(2,1)S(1)}, bf16[512,128]{1,0:T(8,128)(2,1)}, u32[]{:S(2)}) copy-start(bf16[512,128]{1,0:T(8,128)(2,1)} %fusion.54) | copy-start | bytes 393220
  159.5 1.0 copy-start.2
  163.0 29.8 %copy-start.8 = (f32[1,1024]{1,0:T(1,128)S(1)}, f32[1,1024]{1,0:T(1,128)}, u32[]{:S(2)}) copy-start(f32[1,1024]{1,0:T(1,128)} %get-tuple-element.82) | copy-start | bytes 12292
  163.0 29.8 %copy-start.9 = (f32[1,1024]{1,0:T(1,128)S(1)}, f32[1,1024]{1,0:T(1,128)}, u32[]{:S(2)}) copy-start(f32[1,1024]{1,0:T(1,128)} %get-tuple-element.83) | copy-start | bytes 12292
  163.0 29.8 %copy-start.10 = (f32[1,1024]{1,0:T(1,128)S(1)}, f32[1,1024]{1,0:T(1,128)}, u32[]{:S(2)}) copy-start(f32[1,1024]{1,0:T(1,128)} %get-tuple-element.84) | copy-start | bytes 12292
  163.0 29.8 %copy-start.11 = (f32[1,1024]{1,0:T(1,128)S(1)}, f32[1,1024]{1,0:T(1,128)}, u32[]{:S(2)}) copy-start(f32[1,1024]{1,0:T(1,128)} %get-tuple-element.85) | copy-start | bytes 12292
  163.0 29.8 %copy-start.12 = (f32[1,1024]{1,0:T(1,128)S(1)}, f32[1,1024]{1,0:T(1,128)}, u32[]{:S(2)}) copy-start(f32[1,1024]{1,0:T(1,128)} %get-tuple-element.86) | copy-start | bytes 12292
  163.1 29.8 %copy-start.13 = (f32[1,1024]{1,0:T(1,128)S(1)}, f32[1,1024]{1,0:T(1,128)}, u32[]{:S(2)}) copy-start(f32[1,1024]{1,0:T(1,128)} %get-tuple-element.87) | copy-start | bytes 12292
  163.1 29.8 %copy-start.14 = (f32[1,1024]{1,0:T(1,128)S(1)}, f32[1,1024]{1,0:T(1,128)}, u32[]{:S(2)}) copy-start(f32[1,1024]{1,0:T(1,128)} %get-tuple-element.88) | copy-start | bytes 12292
  163.1 29.8 %copy-start.15 = (f32[1,1024]{1,0:T(1,128)S(1)}, f32[1,1024]{1,0:T(1,128)}, u32[]{:S(2)}) copy-start(f32[1,1024]{1,0:T(1,128)} %get-tuple-element.89) | copy-start | bytes 12292
  163.1 29.8 %copy-start.16 = (f32[1,1024]{1,0:T(1,128)S(1)}, f32[1,1024]{1,0:T(1,128)}, u32[]{:S(2)}) copy-start(f32[1,1024]{1,0:T(1,128)} %get-tuple-element.90) | copy-start | bytes 12292
  163.1 29.8 %copy-start.17 = (f32[1,1024]{1,0:T(1,128)S(1)}, f32[1,1024]{1,0:T(1,128)}, u32[]{:S(2)}) copy-start(f32[1,1024]{1,0:T(1,128)} %get-tuple-element.91) | copy-start | bytes 12292
  163.1 29.8 %copy-start.18 = (f32[1,1024]{1,0:T(1,128)S(1)}, f32[1,1024]{1,0:T(1,128)}, u32[]{:S(2)}) copy-start(f32[1,1024]{1,0:T(1,128)} %get-tuple-element.92) | copy-start | bytes 12292
  163.1 29.8 %copy-start.19 = (f32[1,1024]{1,0:T(1,128)S(1)}, f32[1,1024]{1,0:T(1,128)}, u32[]{:S(2)}) copy-start(f32[1,1024]{1,0:T(1,128)} %get-tuple-element.93) | copy-start | bytes 12292
  163.1 29.8 %copy-start.20 = (f32[1,1024]{1,0:T(1,128)S(1)}, f32[1,1024]{1,0:T(1,128)}, u32[]{:S(2)}) copy-start(f32[1,1024]{1,0:T(1,128)} %get-tuple-element.94) | copy-start | bytes 12292
  163.1 29.8 %copy-start.21 = (f32[1,1024]{1,0:T(1,128)S(1)}, f32[1,1024]{1,0:T(1,128)}, u32[]{:S(2)}) copy-start(f32[1,1024]{1,0:T(1,128)} %get-tuple-element.95) | copy-start | bytes 12292
  163.1 29.8 %copy-start.22 = (f32[1,1024]{1,0:T(1,128)S(1)}, f32[1,1024]{1,0:T(1,128)}, u32[]{:S(2)}) copy-start(f32[1,1024]{1,0:T(1,128)} %get-tuple-element.96) | copy-start | bytes 12292
  163.2 29.8 %copy-start.23 = (f32[1,1024]{1,0:T(1,128)S(1)}, f32[1,1024]{1,0:T(1,128)}, u32[]{:S(2)}) copy-start(f32[1,1024]{1,0:T(1,128)} %get-tuple-element.97) | copy-start | bytes 12292
  163.2 29.8 %copy-start.24 = (f32[1,1024]{1,0:T(1,128)S(1)}, f32[1,1024]{1,0:T(1,128)}, u32[]{:S(2)}) copy-start(f32[1,1024]{1,0:T(1,128)} %get-tuple-element.98) | copy-start | bytes 12292
  186.4 6.3 %collective-permute-start.2 = (bf16[15,1024]{1,0:T(8,128)(2,1)S(1)}, bf16[15,1024]{1,0:T(8,128)(2,1)S(1)}, u32[]{:S(2)}, u32[]{:S(2)}) collective-permute-start(bf16[15,1024]{1,0:T(8,128)(2,1)S(1)} %get-tuple-element.62), channel_id=1, source_target_pairs={{0,1},{1,2},{2,3},{3,4},{4,5},{5,6},{6,7},{7,8},{8,9},{9,10},{10,1... | collective-permute-start | bytes 92168 | tf_op jit(solution)/shard_map/ppermute | solution.py:20
  188.8 3.9 %collective-permute-start.3 = (bf16[15,1024]{1,0:T(8,128)(2,1)S(1)}, bf16[15,1024]{1,0:T(8,128)(2,1)S(1)}, u32[]{:S(2)}, u32[]{:S(2)}) collective-permute-start(bf16[15,1024]{1,0:T(8,128)(2,1)S(1)} %get-tuple-element.63), channel_id=1, source_target_pairs={{1,0},{2,1},{3,2},{4,3},{5,4},{6,5},{7,6},{8,7},{9,8},{10,9},{11,1... | collective-permute-start | bytes 92168 | tf_op jit(solution)/shard_map/ppermute | solution.py:21
  193.0 2.8 %copy-start.6 = (f32[1024,512]{1,0:T(8,128)S(1)}, f32[1024,512]{1,0:T(8,128)}, u32[]{:S(2)}) copy-start(f32[1024,512]{1,0:T(8,128)} %get-tuple-element.15) | copy-start | bytes 6291460
  195.7 2.3 %copy-start.5 = (f32[512,1024]{1,0:T(8,128)S(1)}, f32[512,1024]{1,0:T(8,128)}, u32[]{:S(2)}) copy-start(f32[512,1024]{1,0:T(8,128)} %get-tuple-element.16) | copy-start | bytes 6291460
